TPU v7x, 256 devices: a whole 4x4x8 slice. The times are simulated.
256 devices in a mesh: wide: 32 (over x_hi, z, core), narrow: 8 (over y, x_lo).
Axes of the slice: x: 4 (x_hi: 2, x_lo: 2; x = x_hi * 2 + x_lo), y: 4, z: 8, core: 2. Of those that a mesh axis runs over, the one named last changes fastest.
Arguments:
- embeddings: bfloat16 [131072, 1024], P(('wide', 'narrow')), may hold values from -6 to 6
- projection: bfloat16 [1024, 256], replicated, may hold values from -0.1875 to 0.1875
- cluster_id: int32 [131072], P(('wide', 'narrow')), may hold values from 0 to 15, never falling along the last dimension, each value on 1 to 16384 neighbouring positions
Outputs:
- best_match: float32 [131072], P('wide')
Inputs may be any that keep to these rules, and one draw needn't show every extreme that they name: cluster_id never falls along the rows; each cluster holds 1 to 16384 rows, one exactly 16384.
All inputs are finite; a program needn't handle non-finite values.
Results may differ from a plain program's by a relative error of at most 0.00089.
Values may be sent and summed in bfloat16 or wider, within the bound.
A program may use at most 64 MiB of HBM per device.

v0:
```python
import jax
import jax.numpy as jnp
from jax import lax
from jax.sharding import PartitionSpec as P


def passed_along(block, axis, distance):
    devices = range(lax.axis_size(axis))
    route = [((i - distance) % len(devices), i) for i in devices]
    return lax.ppermute(block, axis, route)


def tile_max(best, queries, query_ids, keys, key_ids):
    scores = jnp.dot(queries, keys.T, preferred_element_type=jnp.float32)
    same = query_ids[:, None] == key_ids[None, :]
    return jnp.maximum(best, jnp.max(jnp.where(same, scores, jnp.float32(-1.0)), axis=1))


def body(embeddings, projection, cluster_id):
    sketch = jnp.dot(embeddings, projection, preferred_element_type=jnp.float32)
    squares = jnp.sum(sketch * sketch, axis=1, keepdims=True)
    inverse = lax.rsqrt(squares + 1e-06)
    unit = (sketch * inverse).astype(jnp.bfloat16)
    block_unit, block_ids = (
        lax.all_gather(unit, "narrow", axis=0, tiled=True),
        lax.all_gather(cluster_id, "narrow", axis=0, tiled=True),
    )
    best = jnp.full((unit.shape[0],), -1.0, jnp.float32)
    for offset in (1, 2, -1, -2):
        keys, key_ids = passed_along((block_unit, block_ids), "wide", offset)
        best = tile_max(best, unit, cluster_id, keys, key_ids)
    return lax.all_gather(best, "narrow", axis=0, tiled=True)


def solution(mesh):
    in_specs = (P(("wide", "narrow"), None), P(), P(("wide", "narrow")))
    out_specs = P("wide")
    return jax.shard_map(body, mesh=mesh, in_specs=in_specs, out_specs=out_specs, check_vma=False)
```

profile of v0, /device:TPU:2, one launch (start us, length us, event | category | flops | bytes accessed | tf_op | source)
XLA Modules:
  0.0 212.4 jit_solution(13002550386978463459)
XLA Ops:
  6.5 0.0 copy-start
  6.5 0.0 all-gather.4.cloned.1.call-start
  6.5 1.2 copy-done
  7.8 1.5 multiply_reduce_fusion
  9.3 0.7 multiply_convert_fusion
  10.0 0.0 all-gather.4.cloned.1.call-update
  10.1 56.1 %all-gather.4.cloned.1.call-done = bf16[4096,256]{0,1:T(8,128)(2,1)} async-done(((bf16[512,256]{0,1:T(8,128)(2,1)}), bf16[4096,256]{0,1:T(8,128)(2,1)}) %all-gather.4.cloned.1.call-update) | async-done | bytes 2097168 | tf_op jit(solution)/shard_map/all_gather | solution.py:25
  66.1 4.6 %collective-permute-start.5 = (bf16[4096,256]{0,1:T(8,128)(2,1)}, bf16[4096,256]{0,1:T(8,128)(2,1)S(1)}, u32[]{:S(2)}, u32[]{:S(2)}) collective-permute-start(bf16[4096,256]{0,1:T(8,128)(2,1)} %all-gather.4.cloned.1.call-done), channel_id=1, source_target_pairs={{8,0},{16,8},{24,16},{32,24},{40,32},{48,40},{56,48},{64,56},{72,6... | collective-permute-start | bytes 6291464 | tf_op jit(solution)/shard_map/ppermute | solution.py:10
  70.7 1.4 collective-permute-start.7
  72.1 0.7 collective-permute-start.3
  72.7 0.0 collective-permute-start.1
  72.7 0.0 copy-done.2
  72.7 85.4 %all-gather = s32[8,1,512]{2,1,0:T(1,128)S(1)} all-gather(s32[1,1,512]{2,1,0:T(1,128)S(1)} %bitcast.20), channel_id=1, replica_groups=mesh['wide'=32,'narrow'=8] {'narrow'}, dimensions={0}, use_global_device_ids=true | all-gather | bytes 18432 | tf_op jit(solution)/shard_map/all_gather | solution.py:26
  158.1 0.0 collective-permute-start
  158.1 0.0 collective-permute-done.5
  158.1 0.1 collective-permute-start.2
  158.2 2.2 %fusion.1 = f32[512,4096]{1,0:T(8,128)S(1)} fusion(bf16[512,256]{0,1:T(8,128)(2,1)} %multiply_convert_fusion, bf16[4096,256]{0,1:T(8,128)(2,1)S(1)} %collective-permute-done.5), kind=kOutput, calls=%fused_computation.9 | convolution fusion | flops 1073741824 | bytes 10747904 | tf_op jit(solution)/shard_map/dot_general | solution.py:14
  160.4 0.0 collective-permute-done.7
  160.5 5.4 %collective-permute-start.4 = (s32[4096]{0:T(1024)S(1)}, s32[4096]{0:T(1024)S(1)}, u32[]{:S(2)}, u32[]{:S(2)}) collective-permute-start(s32[4096]{0:T(1024)S(1)} %bitcast.17), channel_id=1, source_target_pairs={{8,0},{16,8},{24,16},{32,24},{40,32},{48,40},{56,48},{64,56},{72,6... | collective-permute-start | bytes 49160 | tf_op jit(solution)/shard_map/ppermute | solution.py:10
  165.8 0.0 copy-done.1
  165.8 1.3 fusion.2
  167.1 0.0 collective-permute-done.3
  167.1 2.0 collective-permute-start.6
  169.1 4.5 %fusion = f32[512,4096]{1,0:T(8,128)} fusion(bf16[512,256]{0,1:T(8,128)(2,1)S(1)} %copy-done.1, bf16[4096,256]{0,1:T(8,128)(2,1)S(1)} %collective-permute-done.3), kind=kOutput, calls=%fused_computation.8 | convolution fusion | flops 1073741824 | bytes 10747904 | tf_op jit(solution)/shard_map/dot_general | solution.py:14
  173.6 0.0 collective-permute-done
  173.6 0.0 collective-permute-done.2
  173.6 0.0 collective-permute-done.4
  173.6 0.0 collective-permute-done.6
  173.6 0.0 collective-permute-done.1
  173.7 6.7 %select_reduce_fusion.3 = (f32[512]{0:T(512)S(1)}, f32[512]{0:T(512)S(1)}, f32[512]{0:T(512)S(1)}, f32[512]{0:T(512)S(1)}) fusion(s32[4096]{0:T(1024)S(1)} %collective-permute-done, s32[512]{0:T(512)S(1)} %copy-done.2, f32[512,4096]{1,0:T(8,128)} %fusion, s32[4096]{0:T(1024)S(1)} %collective-permute-done.2, f32[512,4096]{1,0:T(8,128)S(1)} %fusion.1, ...), kind=kOutput, calls=%fused_computation.3 | convolution fusion | flops 1098905600 | bytes 27600896 | tf_op jit(solution)/shard_map/dot_general | solution.py:14
  180.4 24.6 %all-gather.1 = f32[8,1,512]{2,1,0:T(1,128)S(1)} all-gather(f32[1,1,512]{2,1,0:T(1,128)S(1)} %bitcast.19), channel_id=1, replica_groups=mesh['wide'=32,'narrow'=8] {'narrow'}, dimensions={0}, use_global_device_ids=true | all-gather | bytes 18432 | tf_op jit(solution)/shard_map/all_gather | solution.py:32
  205.0 0.6 copy.5
  (4 shorter events, 0.0 us)
Async XLA Ops:
  6.5 1.2 copy-start
  6.5 66.2 %copy-start.2 = (s32[512]{0:T(512)S(1)}, s32[512]{0:T(512)}, u32[]{:S(2)}) copy-start(s32[512]{0:T(512)} %param.5) | copy-start | bytes 6148
  6.5 59.6 %all-gather.4.cloned.1.call-start = ((), (), s32[]{:S(2)}) async-start(), calls=%async_computation | async-start | bytes 2359296 | tf_op jit(solution)/shard_map/all_gather | solution.py:25
  66.1 92.0 %collective-permute-start.5 = (bf16[4096,256]{0,1:T(8,128)(2,1)}, bf16[4096,256]{0,1:T(8,128)(2,1)S(1)}, u32[]{:S(2)}, u32[]{:S(2)}) collective-permute-start(bf16[4096,256]{0,1:T(8,128)(2,1)} %all-gather.4.cloned.1.call-done), channel_id=1, source_target_pairs={{8,0},{16,8},{24,16},{32,24},{40,32},{48,40},{56,48},{64,56},{72,6... | collective-permute-start | bytes 6291464 | tf_op jit(solution)/shard_map/ppermute | solution.py:10
  70.7 89.8 %collective-permute-start.7 = (bf16[4096,256]{0,1:T(8,128)(2,1)}, bf16[4096,256]{0,1:T(8,128)(2,1)S(1)}, u32[]{:S(2)}, u32[]{:S(2)}) collective-permute-start(bf16[4096,256]{0,1:T(8,128)(2,1)} %all-gather.4.cloned.1.call-done), channel_id=1, source_target_pairs={{16,0},{24,8},{32,16},{40,24},{48,32},{56,40},{64,48},{72,56},{80,... | collective-permute-start | bytes 6291464 | tf_op jit(solution)/shard_map/ppermute | solution.py:10
  72.1 95.0 %collective-permute-start.3 = (bf16[4096,256]{0,1:T(8,128)(2,1)}, bf16[4096,256]{0,1:T(8,128)(2,1)S(1)}, u32[]{:S(2)}, u32[]{:S(2)}) collective-permute-start(bf16[4096,256]{0,1:T(8,128)(2,1)} %all-gather.4.cloned.1.call-done), channel_id=1, source_target_pairs={{240,0},{248,8},{0,16},{8,24},{16,32},{24,40},{32,48},{40,56},{48,... | collective-permute-start | bytes 6291464 | tf_op jit(solution)/shard_map/ppermute | solution.py:10
  72.7 100.9 %collective-permute-start.1 = (bf16[4096,256]{0,1:T(8,128)(2,1)}, bf16[4096,256]{0,1:T(8,128)(2,1)S(1)}, u32[]{:S(2)}, u32[]{:S(2)}) collective-permute-start(bf16[4096,256]{0,1:T(8,128)(2,1)} %all-gather.4.cloned.1.call-done), channel_id=1, source_target_pairs={{248,0},{0,8},{8,16},{16,24},{24,32},{32,40},{40,48},{48,56},{56,6... | collective-permute-start | bytes 6291464 | tf_op jit(solution)/shard_map/ppermute | solution.py:10
  158.1 7.7 %copy-start.1 = (bf16[512,256]{0,1:T(8,128)(2,1)S(1)}, bf16[512,256]{0,1:T(8,128)(2,1)}, u32[]{:S(2)}) copy-start(bf16[512,256]{0,1:T(8,128)(2,1)} %multiply_convert_fusion) | copy-start | bytes 786436
  158.1 15.5 %collective-permute-start = (s32[4096]{0:T(1024)S(1)}, s32[4096]{0:T(1024)S(1)}, u32[]{:S(2)}, u32[]{:S(2)}) collective-permute-start(s32[4096]{0:T(1024)S(1)} %bitcast.15), channel_id=1, source_target_pairs={{248,0},{0,8},{8,16},{16,24},{24,32},{32,40},{40,48},{48,56},{56,6... | collective-permute-start | bytes 49160 | tf_op jit(solution)/shard_map/ppermute | solution.py:10
  158.1 15.5 %collective-permute-start.2 = (s32[4096]{0:T(1024)S(1)}, s32[4096]{0:T(1024)S(1)}, u32[]{:S(2)}, u32[]{:S(2)}) collective-permute-start(s32[4096]{0:T(1024)S(1)} %bitcast.16), channel_id=1, source_target_pairs={{240,0},{248,8},{0,16},{8,24},{16,32},{24,40},{32,48},{40,56},{48,... | collective-permute-start | bytes 49160 | tf_op jit(solution)/shard_map/ppermute | solution.py:10
  160.5 13.2 %collective-permute-start.4 = (s32[4096]{0:T(1024)S(1)}, s32[4096]{0:T(1024)S(1)}, u32[]{:S(2)}, u32[]{:S(2)}) collective-permute-start(s32[4096]{0:T(1024)S(1)} %bitcast.17), channel_id=1, source_target_pairs={{8,0},{16,8},{24,16},{32,24},{40,32},{48,40},{56,48},{64,56},{72,6... | collective-permute-start | bytes 49160 | tf_op jit(solution)/shard_map/ppermute | solution.py:10
  167.1 6.5 %collective-permute-start.6 = (s32[4096]{0:T(1024)S(1)}, s32[4096]{0:T(1024)S(1)}, u32[]{:S(2)}, u32[]{:S(2)}) collective-permute-start(s32[4096]{0:T(1024)S(1)} %bitcast.18), channel_id=1, source_target_pairs={{16,0},{24,8},{32,16},{40,24},{48,32},{56,40},{64,48},{72,56},{80,... | collective-permute-start | bytes 49160 | tf_op jit(solution)/shard_map/ppermute | solution.py:10
Sparse Core Ops, SparseCore 0:
  10.2 55.8 all-gather.3
where the time goes:
time: 214 us; the launch traced here: 212 us
  blocking collectives  110 us (51%)
  waiting for transfers between devices  56.1 us (26%)
  matrix products  16.3 us (8%)
  starting transfers between devices  14 us (7%)
  between operations  13.5 us (6%)
    all_gather x1, blocking collectives, body(): lax.all_gather(cluster_id, 'narrow', axis=0, tiled=True)  85.4 us
    all_gather x1, waiting for transfers between devices, body(): lax.all_gather(unit, 'narrow', axis=0, tiled=True)  56.1 us
    all_gather x1, blocking collectives, body(): return lax.all_gather(best, 'narrow', axis=0, tiled=True)  24.6 us
    dot_general x4, matrix products, tile_max(): scores = jnp.dot(queries, keys.T, preferred_element_type=jnp.float32)  14.8 us
    ppermute x8, starting transfers between devices, passed_along(): return lax.ppermute(block, axis, route)  14 us
  transfers between devices with their start and end apart: 9, of which 1 were waited for; matrix products, arithmetic and copies ran while one was open for 4% of the time, Pallas kernels for 0%

commit v1 on v0

v1 whole, which is shorter than its diff:
```python
import jax
import jax.numpy as jnp
from jax import lax
from jax.experimental import pallas as pl
from jax.experimental.pallas import tpu as pltpu
from jax.sharding import PartitionSpec as P

MESH = pl.DeviceIdType.MESH
ROWS = 512
SK = 256
D = 1024
CHUNKS = 2
CH = ROWS // CHUNKS
PLANES = 16
LANES = 128
GROUPS = ROWS // LANES


def device(plane, n, core):
    return (lax.rem(plane + PLANES, PLANES) * 2 + core, n)


def kernel(
    emb,
    proj,
    ids,
    out,
    emb_v,
    proj_v,
    r_unit,
    s_unit,
    r_ids,
    s_ids,
    r_col,
    row_acc,
    col_acc,
    row_all,
    col_src,
    col_all,
    in_sem,
    y_send,
    r_recv,
    s_send,
    s_recv,
    f_send,
    id_send,
    rid_recv,
    sid_recv,
    tail_send,
    tail_recv,
):
    wide, n = lax.axis_index("wide"), lax.axis_index("narrow")
    plane, core = wide // 2, lax.rem(wide, 2)
    y, x = n // 2, lax.rem(n, 2)
    n_x = y * 2 + 1 - x

    proj_in = pltpu.make_async_copy(proj, proj_v, in_sem.at[CHUNKS])
    proj_in.start()
    emb_in = []
    for k in range(CHUNKS):
        rows = pl.ds(k * CH, CH)
        emb_in.append(pltpu.make_async_copy(emb.at[rows], emb_v.at[rows], in_sem.at[k]))
        emb_in[k].start()

    barrier = pltpu.get_barrier_semaphore()

    def greet(where):
        pl.semaphore_signal(barrier, inc=1, device_id=where, device_id_type=MESH)

    for k in range(1, 8):
        greet(device(plane, lax.rem(n + k, 8), core))
    for k in range(8):
        greet(device(plane - 1 + core, k, 0))
        greet(device(plane - 1 + 2 * core, k, 1))
    for m in (n, n_x):
        greet(device(plane + 1, m, 0))
        greet(device(plane - core, m, 1))

    def y_peer(k):
        return device(plane, lax.rem(y + k, 4) * 2 + x, core)

    def unit_copy(k, to_slot, buf, send, recv, where):
        rows = pl.ds(k * CH, CH)
        return pltpu.make_async_remote_copy(
            src_ref=r_unit.at[0, rows],
            dst_ref=buf.at[to_slot, rows],
            send_sem=send,
            recv_sem=recv.at[to_slot, k],
            device_id=where,
            device_id_type=MESH,
        )

    def y_copies(k):
        return [
            unit_copy(k, 4 - d, r_unit, y_send.at[d - 1, k], r_recv, y_peer(d))
            for d in (2, 1, 3)
        ]

    def s_copies_0(k):
        return [
            unit_copy(k, 3, s_unit, s_send.at[1, k], s_recv, device(plane - 1, n_x, 0)),
            unit_copy(k, 2, s_unit, s_send.at[0, k], s_recv, device(plane - 1, n, 0)),
        ]

    def s_copies_1(k):
        return [
            unit_copy(k, 1, s_unit, s_send.at[3, k], s_recv, device(plane + 1, n_x, 1)),
            unit_copy(k, 0, s_unit, s_send.at[2, k], s_recv, device(plane + 1, n, 1)),
            unit_copy(k, 1, s_unit, s_send.at[1, k], s_recv, device(plane, n_x, 0)),
            unit_copy(k, 0, s_unit, s_send.at[0, k], s_recv, device(plane, n, 0)),
        ]

    def id_copy(to_slot, buf, send, recv, where):
        return pltpu.make_async_remote_copy(
            src_ref=ids,
            dst_ref=buf.at[to_slot],
            send_sem=send,
            recv_sem=recv.at[to_slot],
            device_id=where,
            device_id_type=MESH,
        )

    def id_copies_y():
        return [id_copy(4 - d, r_ids, id_send.at[d - 1], rid_recv, y_peer(d)) for d in (2, 1, 3)]

    def id_copies_0():
        return [
            id_copy(slot, s_ids, id_send.at[3 + 2 * c + i], sid_recv, device(plane - 1, m, c))
            for c in (0, 1)
            for i, (slot, m) in enumerate(((2, n), (3, n_x)))
        ]

    def id_copies_1():
        return [
            id_copy(slot, s_ids, id_send.at[3 + 2 * c + i], sid_recv, device(plane + c, m, c))
            for c in (0, 1)
            for i, (slot, m) in enumerate(((0, n), (1, n_x)))
        ]

    def start(copies):
        for copy in copies:
            copy.start()

    def by_core(of_0, of_1, act):
        @pl.when(core == 0)
        def _():
            for copy in of_0():
                act(copy)

        @pl.when(core == 1)
        def _():
            for copy in of_1():
                act(copy)

    proj_in.wait()
    for k in range(CHUNKS):
        emb_in[k].wait()
        sketch = jnp.dot(
            emb_v[k * CH : (k + 1) * CH, :], proj_v[...], preferred_element_type=jnp.float32
        )
        squares = jnp.sum(sketch * sketch, axis=1, keepdims=True)
        unit = (sketch * lax.rsqrt(squares + 1e-06)).astype(jnp.bfloat16)
        r_unit[0, k * CH : (k + 1) * CH, :] = unit
        if k == 0:
            pl.semaphore_wait(barrier, 27)
        start(y_copies(k))
        by_core(lambda: s_copies_0(k), lambda: s_copies_1(k), lambda c: c.start())
        if k == 0:
            start(id_copies_y())
            by_core(id_copies_0, id_copies_1, lambda c: c.start())

    def columns(slot, rows):
        for j in range(GROUPS):
            row = rows[j : j + 1, :].astype(jnp.float32)
            r_col[slot, j * LANES : (j + 1) * LANES, :] = jnp.broadcast_to(row, (LANES, LANES)).T

    columns(0, ids[...])
    row_acc[...] = jnp.full_like(row_acc, -1.0)
    col_acc[...] = jnp.full_like(col_acc, -1.0)

    def tiles(r, k, slots):
        rows = pl.ds(pl.multiple_of(k * CH, CH), CH)
        a = r_unit[r, rows, :]
        a_ids = r_col[r, rows, :]
        best = row_acc[rows, :]
        for s in slots:
            scores = lax.dot_general(
                a, s_unit[s], (((1,), (1,)), ((), ())), preferred_element_type=jnp.float32
            )
            for j in range(GROUPS):
                lanes = slice(j * LANES, (j + 1) * LANES)
                b_ids = s_ids[s, j : j + 1, :].astype(jnp.float32)
                kept = jnp.where(a_ids == b_ids, scores[:, lanes], -1.0)
                best = jnp.maximum(best, kept)
                peak = jnp.max(kept.reshape(CH // 8, 8, LANES), axis=0)
                col_acc[s, :, lanes] = jnp.maximum(col_acc[s, :, lanes], peak)
        row_acc[rows, :] = best

    def rows_done(r):
        y_abs = lax.rem(y + r, 4)
        for j in range(GROUPS):
            part = row_acc[j * LANES : (j + 1) * LANES, :].T
            row_all[n, y_abs, j : j + 1, :] = jnp.max(part, axis=0, keepdims=True)
        if r != 2:
            row_acc[...] = jnp.full_like(row_acc, -1.0)

    def s_wait(s, k):
        rows = pl.ds(k * CH, CH)
        pltpu.make_async_copy(s_unit.at[s, rows], s_unit.at[s, rows], s_recv.at[s, k]).wait()

    def forward(s, k):
        rows = pl.ds(k * CH, CH)
        return pltpu.make_async_remote_copy(
            src_ref=s_unit.at[s, rows],
            dst_ref=s_unit.at[s, rows],
            send_sem=f_send.at[s - 2, k],
            recv_sem=s_recv.at[s, k],
            device_id=device(plane, n, 1),
            device_id_type=MESH,
        )

    def id_wait(buf, slot, recv):
        pltpu.make_async_copy(buf.at[slot], buf.at[slot], recv.at[slot]).wait()

    for s in range(4):
        id_wait(s_ids, s, sid_recv)
        for k in range(CHUNKS):
            s_wait(s, k)
            if s >= 2:

                @pl.when(core == 0)
                def _():
                    forward(s, k).start()

        @pl.loop(0, CHUNKS)
        def _(k):
            tiles(0, k, (s,))

    rows_done(0)
    for r in (1, 3, 2):
        id_wait(r_ids, r, rid_recv)
        columns(r, r_ids[r])

        @pl.loop(0, CHUNKS)
        def _(k):
            rows = pl.ds(pl.multiple_of(k * CH, CH), CH)
            pltpu.make_async_copy(r_unit.at[r, rows], r_unit.at[r, rows], r_recv.at[r, k]).wait()
            tiles(r, k, range(4))

        rows_done(r)

    for s in range(4):
        x_abs = x if s % 2 == 0 else 1 - x
        for j in range(GROUPS):
            col_src[s // 2, x_abs, j : j + 1, :] = jnp.max(
                col_acc[s, :, j * LANES : (j + 1) * LANES], axis=0, keepdims=True
            )

    def tail(src, dst, kind, where):
        return pltpu.make_async_remote_copy(
            src_ref=src,
            dst_ref=dst,
            send_sem=tail_send.at[kind],
            recv_sem=tail_recv.at[kind],
            device_id=where,
            device_id_type=MESH,
        )

    for k in range(8):
        tail(col_src.at[1], col_all.at[core, n], 1, device(plane + 1, k, 0)).start()
    for k in range(8):
        tail(col_src.at[0], col_all.at[core, n], 1, device(plane - core, k, 1)).start()
    for k in range(1, 8):
        tail(row_all.at[n], row_all.at[n], 0, device(plane, lax.rem(n + k, 8), core)).start()

    some = row_all.at[pl.ds(0, 7)]
    pltpu.make_async_copy(some, some, tail_recv.at[0]).wait()
    pltpu.make_async_copy(col_all, col_all, tail_recv.at[1]).wait()
    for y_abs in range(4):
        for x_abs in range(2):
            best = jnp.full((GROUPS, LANES), -1.0, jnp.float32)
            for y_from in range(4):
                best = jnp.maximum(best, row_all[y_from * 2 + x_abs, y_abs])
            for c in range(2):
                for x_from in range(2):
                    best = jnp.maximum(best, col_all[c, y_abs * 2 + x_from, x_abs])
            out[y_abs * 2 + x_abs] = best

    pltpu.make_async_copy(some, some, tail_send.at[0]).wait()
    pltpu.make_async_copy(col_all, col_all, tail_send.at[1]).wait()
    for k in range(CHUNKS):
        for copy in y_copies(k):
            copy.wait_send()
        by_core(lambda: s_copies_0(k), lambda: s_copies_1(k), lambda c: c.wait_send())
        for s in (2, 3):

            @pl.when(core == 0)
            def _():
                forward(s, k).wait_send()

    for copy in id_copies_y():
        copy.wait_send()
    by_core(id_copies_0, id_copies_1, lambda c: c.wait_send())


def body(embeddings, projection, cluster_id):
    dma = pltpu.SemaphoreType.DMA
    best = pl.pallas_call(
        kernel,
        out_shape=jax.ShapeDtypeStruct((8, GROUPS, LANES), jnp.float32),
        in_specs=[
            pl.BlockSpec(memory_space=pl.ANY),
            pl.BlockSpec(memory_space=pl.ANY),
            pl.BlockSpec(memory_space=pltpu.VMEM),
        ],
        out_specs=pl.BlockSpec(memory_space=pltpu.VMEM),
        scratch_shapes=[
            pltpu.VMEM((ROWS, D), jnp.bfloat16),
            pltpu.VMEM((D, SK), jnp.bfloat16),
            pltpu.VMEM((4, ROWS, SK), jnp.bfloat16),
            pltpu.VMEM((4, ROWS, SK), jnp.bfloat16),
            pltpu.VMEM((4, GROUPS, LANES), jnp.int32),
            pltpu.VMEM((4, GROUPS, LANES), jnp.int32),
            pltpu.VMEM((4, ROWS, LANES), jnp.float32),
            pltpu.VMEM((ROWS, LANES), jnp.float32),
            pltpu.VMEM((4, 8, ROWS), jnp.float32),
            pltpu.VMEM((8, 4, GROUPS, LANES), jnp.float32),
            pltpu.VMEM((2, 2, GROUPS, LANES), jnp.float32),
            pltpu.VMEM((2, 8, 2, GROUPS, LANES), jnp.float32),
            dma((CHUNKS + 1,)),
            dma((3, CHUNKS)),
            dma((4, CHUNKS)),
            dma((4, CHUNKS)),
            dma((4, CHUNKS)),
            dma((2, CHUNKS)),
            dma((7,)),
            dma((4,)),
            dma((4,)),
            dma((2,)),
            dma((2,)),
        ],
        compiler_params=pltpu.CompilerParams(
            collective_id=0, has_side_effects=True, vmem_limit_bytes=62 << 20
        ),
        name="best_match",
    )(embeddings, projection, cluster_id.reshape(GROUPS, LANES))
    return best.reshape(8 * ROWS)


def solution(mesh):
    in_specs = (P(("wide", "narrow"), None), P(), P(("wide", "narrow")))
    out_specs = P("wide")
    return jax.shard_map(body, mesh=mesh, in_specs=in_specs, out_specs=out_specs, check_vma=False)
```

time: 214 us -> 34.6 us (0.16)
  blocking collectives: 110 us -> 0 us
  waiting for transfers between devices: 56.1 us -> 0 us
  Pallas kernels: 0 us -> 32.6 us
  matrix products: 16.3 us -> 0 us
  starting transfers between devices: 14 us -> 0 us
  between operations: 13.5 us -> 0.01 us
    all_gather x2 -> x0, blocking collectives: 110 us -> none  [the longest x1 85.4 us: body(): lax.all_gather(cluster_id, 'narrow', axis=0, tiled=True)]
    all_gather x1 -> x0, waiting for transfers between devices: 56.1 us -> none  [body(): lax.all_gather(unit, 'narrow', axis=0, tiled=True)]
    pallas_call x0 -> x1, Pallas kernels: none -> 32.6 us  [body(): pl.pallas_call(kernel, out_shape=jax.ShapeDtypeStruct((8, GROUPS, LANES),...]
    dot_general x5 -> x0, matrix products: 16.3 us -> none  [the longest x4 14.8 us: tile_max(): scores = jnp.dot(queries, keys.T, preferred_element_type=jnp.float32)]
    ppermute x8 -> x0, starting transfers between devices: 14 us -> none  [passed_along(): return lax.ppermute(block, axis, route)]
  transfers between devices with their start and end apart: 9 -> 0, of which waited for: 1 -> 0; matrix products, arithmetic and copies ran while one was open for 4% -> 0% of each run, Pallas kernels for 0% -> 0%
where the time goes in v1:
time: 34.6 us; the launch traced here: 33.9 us
  Pallas kernels  32.6 us (94%)
  local copies, waits for them, and re-layouts  1.32 us (4%)
    pallas_call x1, Pallas kernels, body(): pl.pallas_call(kernel, out_shape=jax.ShapeDtypeStruct((8, GROUPS, LANES),...  32.6 us
    unnamed x1, local copies, waits for them, and re-layouts  1.32 us

profile of v1, /device:TPU:2, one launch (start us, length us, event | category | flops | bytes accessed | tf_op | source)
XLA Modules:
  0.0 33.9 jit_solution(12535712680568215895)
XLA Ops:
  0.0 32.6 %best_match.1 = f32[8,4,128]{2,1,0:T(4,128)} custom-call(bf16[512,1024]{1,0:T(8,128)(2,1)} %emb.1, bf16[1024,256]{1,0:T(8,128)(2,1)} %proj.1, s32[4,128]{1,0:T(4,128)} %bitcast.3), custom_call_target="tpu_custom_call" | custom-call | tf_op jit(solution)/shard_map/best_match/pallas_call | solution.py:308
  32.6 1.3 %copy.5 = f32[4096]{0:T(1024)} copy(f32[4096]{0:T(1024)} %bitcast.2) | data formatting | bytes 32768

commit v2 on v0

v2 whole, which is shorter than its diff:
```python
import jax
import jax.numpy as jnp
from jax import lax
from jax.experimental import pallas as pl
from jax.experimental.pallas import tpu as pltpu
from jax.sharding import PartitionSpec as P

MESH = pl.DeviceIdType.MESH
ROWS = 512
SK = 256
D = 1024
CHUNKS = 4
CH = ROWS // CHUNKS
HALF = ROWS // 2
PLANES = 16
LANES = 128
GROUPS = ROWS // LANES


def device(plane, n, core):
    return (lax.rem(plane + PLANES, PLANES) * 2 + core, n)


def kernel(
    emb,
    proj,
    ids,
    out,
    emb_v,
    proj_v,
    r_unit,
    s_unit,
    r_ids,
    s_ids,
    r_col,
    row_acc,
    col_acc,
    row_all,
    col_src,
    col_all,
    in_sem,
    y_send,
    relay_send,
    r_recv,
    p_send,
    f_send,
    q_send,
    s_recv,
    id_send,
    rid_recv,
    sid_recv,
    tail_send,
    tail_recv,
):
    wide, n = lax.axis_index("wide"), lax.axis_index("narrow")
    plane, core = wide // 2, lax.rem(wide, 2)
    y, x = n // 2, lax.rem(n, 2)
    n_x = y * 2 + 1 - x
    crosses_out = lax.rem(plane, 8) == 7
    crosses_in = lax.rem(plane, 8) == 0
    n_p = jnp.where(crosses_out, n_x, n)
    n_f = jnp.where(crosses_out, n, n_x)
    x_p = jnp.where(crosses_in, 1 - x, x)
    x_q = jnp.where(core == 0, x_p, x)

    proj_in = pltpu.make_async_copy(proj, proj_v, in_sem.at[2])
    proj_in.start()
    emb_in = []
    for h in range(2):
        rows = pl.ds(h * HALF, HALF)
        emb_in.append(pltpu.make_async_copy(emb.at[rows], emb_v.at[rows], in_sem.at[h]))
        emb_in[h].start()

    barrier = pltpu.get_barrier_semaphore()

    def greet(where):
        pl.semaphore_signal(barrier, inc=1, device_id=where, device_id_type=MESH)

    for m in (n, n_x):
        greet(device(plane - 1, m, core))
        greet(device(plane - 1 + core, m, 1 - core))
    for k in range(1, 8):
        greet(device(plane, lax.rem(n + k, 8), core))
    for k in range(8):
        greet(device(plane + 1, k, core))
        greet(device(plane + core, k, 1 - core))

    def remote(src, dst, send, recv, where):
        return pltpu.make_async_remote_copy(
            src_ref=src,
            dst_ref=dst,
            send_sem=send,
            recv_sem=recv,
            device_id=where,
            device_id_type=MESH,
        )

    def piece(k):
        return pl.ds(k * CH, CH)

    def y_peer(d):
        return device(plane, lax.rem(y + d, 4) * 2 + x, core)

    def y_copy(d, k):
        src, dst = r_unit.at[0, piece(k)], r_unit.at[4 - d, piece(k)]
        return remote(src, dst, y_send.at[d // 2, k], r_recv.at[4 - d, k], y_peer(d))

    def relay_copy(d, k):
        src, dst = r_unit.at[d, piece(k)], r_unit.at[2, piece(k)]
        return remote(src, dst, relay_send.at[d // 2, k % 2], r_recv.at[2, k], y_peer(4 - d))

    def p_copy(k):
        src, dst = r_unit.at[0, piece(k)], s_unit.at[0, piece(k)]
        return remote(src, dst, p_send.at[k], s_recv.at[0, k], device(plane + 1, n_p, core))

    def f_copy(k):
        src, dst = s_unit.at[0, piece(k)], s_unit.at[1, piece(k)]
        return remote(src, dst, f_send.at[k], s_recv.at[1, k], device(plane, n_x, core))

    def q0_copy(i, k):
        src, dst = r_unit.at[0, piece(k)], s_unit.at[2 + i, piece(k)]
        where = device(plane, n_x if i else n, 1)
        return remote(src, dst, q_send.at[i, k], s_recv.at[2 + i, k], where)

    def q1_copy(i, k):
        src, dst = s_unit.at[i, piece(k)], s_unit.at[2 + i, piece(k)]
        return remote(src, dst, q_send.at[i, k], s_recv.at[2 + i, k], device(plane, n, 0))

    def id_copies():
        copies = [
            remote(ids, r_ids.at[4 - d], id_send.at[d - 1], rid_recv.at[4 - d], y_peer(d))
            for d in (2, 1, 3)
        ]
        n_q = jnp.where(core == 0, n, n_p)
        n_r = jnp.where(core == 0, n_x, n_f)
        for slot, where in enumerate(
            (
                device(plane + 1, n_p, core),
                device(plane + 1, n_f, core),
                device(plane + core, n_q, 1 - core),
                device(plane + core, n_r, 1 - core),
            )
        ):
            copies.append(remote(ids, s_ids.at[slot], id_send.at[3 + slot], sid_recv.at[slot], where))
        return copies

    proj_in.wait()
    for h in range(2):
        emb_in[h].wait()
        rows = slice(h * HALF, (h + 1) * HALF)
        sketch = jnp.dot(emb_v[rows, :], proj_v[...], preferred_element_type=jnp.float32)
        squares = jnp.sum(sketch * sketch, axis=1, keepdims=True)
        r_unit[0, rows, :] = (sketch * lax.rsqrt(squares + 1e-06)).astype(jnp.bfloat16)
        if h == 0:
            pl.semaphore_wait(barrier, 27)
        near = (2 * h, 2 * h + 1)
        for k in near:
            p_copy(k).start()
            y_copy(1, k).start()
            if h == 1:
                y_copy(3, k).start()

        @pl.when(core == 0)
        def _():
            for k in near:
                q0_copy(1, k).start()
                q0_copy(0, k).start()

        if h == 0:
            y_copy(3, 0).start()
            for copy in id_copies():
                copy.start()
        else:
            y_copy(3, 1).start()

    def columns(slot, rows):
        for j in range(GROUPS):
            row = rows[j : j + 1, :].astype(jnp.float32)
            r_col[slot, j * LANES : (j + 1) * LANES, :] = jnp.broadcast_to(row, (LANES, LANES)).T

    columns(0, ids[...])
    row_acc[...] = jnp.full_like(row_acc, -1.0)
    col_acc[...] = jnp.full_like(col_acc, -1.0)

    def landed(ref, sem):
        pltpu.make_async_copy(ref, ref, sem).wait()

    def r_wait(d, k):
        landed(r_unit.at[d, piece(k)], r_recv.at[d, k])

    def s_wait(s, k):
        landed(s_unit.at[s, piece(k)], s_recv.at[s, k])

    def to_core_0(i, k):
        @pl.when(core == 1)
        def _():
            q1_copy(i, k).start()

    for k in range(CHUNKS):
        if k < 2:
            for d, piece_of in ((1, 2 + k), (3, k)):
                r_wait(d, piece_of)
                relay_copy(d, piece_of).start()
        s_wait(0, k)
        f_copy(k).start()
        to_core_0(0, k)

    for d in (1, 3, 2):
        landed(r_ids.at[d], rid_recv.at[d])
        columns(d, r_ids[d])
    for s in range(4):
        landed(s_ids.at[s], sid_recv.at[s])
    for k in range(2):
        r_wait(1, k)
        r_wait(3, 2 + k)

    def tiles(s, blocks, where):
        def step(b, peaks):
            r, rows = where(b)
            scores = lax.dot_general(
                r_unit[r, rows, :],
                s_unit[s],
                (((1,), (1,)), ((), ())),
                preferred_element_type=jnp.float32,
            )
            a_ids = r_col[r, rows, :]
            best = row_acc[r, rows, :]
            new = []
            for j in range(GROUPS):
                b_ids = s_ids[s, j : j + 1, :].astype(jnp.float32)
                kept = jnp.where(a_ids == b_ids, scores[:, j * LANES : (j + 1) * LANES], -1.0)
                best = jnp.maximum(best, kept)
                peak = jnp.max(kept.reshape(HALF // 8, 8, LANES), axis=0)
                new.append(jnp.maximum(peaks[j], peak))
            row_acc[r, rows, :] = best
            return tuple(new)

        peaks = tuple(col_acc[s, j] for j in range(GROUPS))
        peaks = lax.fori_loop(0, blocks, step, peaks)
        for j in range(GROUPS):
            col_acc[s, j] = peaks[j]

    def rows_of(b):
        return pl.ds(pl.multiple_of(lax.rem(b, 2) * HALF, HALF), HALF)

    def near_blocks(b):
        t = b // 2
        return t + t // 2, rows_of(b)

    def far_blocks(b):
        return 2, rows_of(b)

    def all_blocks(b):
        return b // 2, rows_of(b)

    def slot(of_0, of_1):
        return jnp.where(core == 0, of_0, of_1)

    def s_wait_all(s):
        for k in range(CHUNKS):
            s_wait(s, k)

    @pl.when(core == 1)
    def _():
        s_wait_all(2)

    tiles(slot(0, 2), 6, near_blocks)

    @pl.when(core == 0)
    def _():
        s_wait_all(2)

    @pl.when(core == 1)
    def _():
        s_wait_all(3)
        for k in (0, 1):
            s_wait(1, k)
            q1_copy(1, k).start()

    tiles(slot(2, 3), 6, near_blocks)

    for k in range(CHUNKS):
        r_wait(2, k)

    @pl.when(core == 1)
    def _():
        for k in (2, 3):
            s_wait(1, k)
            q1_copy(1, k).start()

    tiles(slot(0, 2), 2, far_blocks)
    tiles(slot(2, 3), 2, far_blocks)

    @pl.when(core == 0)
    def _():
        s_wait_all(1)

    tiles(slot(1, 0), 8, all_blocks)

    @pl.when(core == 0)
    def _():
        s_wait_all(3)

    tiles(slot(3, 1), 8, all_blocks)

    for s in range(4):
        x_abs = (x_p, 1 - x_p, x_q, 1 - x_q)[s]
        for j in range(GROUPS):
            col_src[s // 2, x_abs, j : j + 1, :] = jnp.max(col_acc[s, j], axis=0, keepdims=True)

    def tail(src, dst, kind, where):
        return remote(src, dst, tail_send.at[kind], tail_recv.at[kind], where)

    for k in range(8):
        tail(col_src.at[0], col_all.at[0, n], 1, device(plane - 1, k, core)).start()
        tail(col_src.at[1], col_all.at[1, n], 1, device(plane - 1 + core, k, 1 - core)).start()

    for r in range(4):
        y_abs = lax.rem(y + r, 4)
        for j in range(GROUPS):
            part = row_acc[r, j * LANES : (j + 1) * LANES, :].T
            row_all[n, y_abs, j : j + 1, :] = jnp.max(part, axis=0, keepdims=True)
    for k in range(1, 8):
        tail(row_all.at[n], row_all.at[n], 0, device(plane, lax.rem(n + k, 8), core)).start()

    some = row_all.at[pl.ds(0, 7)]
    landed(some, tail_recv.at[0])
    landed(col_all, tail_recv.at[1])
    for y_abs in range(4):
        for x_abs in range(2):
            best = jnp.full((GROUPS, LANES), -1.0, jnp.float32)
            for y_from in range(4):
                best = jnp.maximum(best, row_all[y_from * 2 + x_abs, y_abs])
            for g in range(2):
                for x_from in range(2):
                    best = jnp.maximum(best, col_all[g, y_abs * 2 + x_from, x_abs])
            out[y_abs * 2 + x_abs] = best

    landed(some, tail_send.at[0])
    landed(col_all, tail_send.at[1])
    for k in range(CHUNKS):
        y_copy(1, k).wait_send()
        y_copy(3, k).wait_send()
        relay_copy(1 if k >= 2 else 3, k).wait_send()
        p_copy(k).wait_send()
        f_copy(k).wait_send()
        for i in range(2):
            landed(r_unit.at[0, piece(k)], q_send.at[i, k])
    for copy in id_copies():
        copy.wait_send()


def body(embeddings, projection, cluster_id):
    dma = pltpu.SemaphoreType.DMA
    best = pl.pallas_call(
        kernel,
        out_shape=jax.ShapeDtypeStruct((8, GROUPS, LANES), jnp.float32),
        in_specs=[
            pl.BlockSpec(memory_space=pl.ANY),
            pl.BlockSpec(memory_space=pl.ANY),
            pl.BlockSpec(memory_space=pltpu.VMEM),
        ],
        out_specs=pl.BlockSpec(memory_space=pltpu.VMEM),
        scratch_shapes=[
            pltpu.VMEM((ROWS, D), jnp.bfloat16),
            pltpu.VMEM((D, SK), jnp.bfloat16),
            pltpu.VMEM((4, ROWS, SK), jnp.bfloat16),
            pltpu.VMEM((4, ROWS, SK), jnp.bfloat16),
            pltpu.VMEM((4, GROUPS, LANES), jnp.int32),
            pltpu.VMEM((4, GROUPS, LANES), jnp.int32),
            pltpu.VMEM((4, ROWS, LANES), jnp.float32),
            pltpu.VMEM((4, ROWS, LANES), jnp.float32),
            pltpu.VMEM((4, GROUPS, 8, LANES), jnp.float32),
            pltpu.VMEM((8, 4, GROUPS, LANES), jnp.float32),
            pltpu.VMEM((2, 2, GROUPS, LANES), jnp.float32),
            pltpu.VMEM((2, 8, 2, GROUPS, LANES), jnp.float32),
            dma((3,)),
            dma((2, CHUNKS)),
            dma((2, 2)),
            dma((4, CHUNKS)),
            dma((CHUNKS,)),
            dma((CHUNKS,)),
            dma((2, CHUNKS)),
            dma((4, CHUNKS)),
            dma((7,)),
            dma((4,)),
            dma((4,)),
            dma((2,)),
            dma((2,)),
        ],
        compiler_params=pltpu.CompilerParams(
            collective_id=0, has_side_effects=True, vmem_limit_bytes=62 << 20
        ),
        name="best_match",
    )(embeddings, projection, cluster_id.reshape(GROUPS, LANES))
    return best.reshape(8 * ROWS)


def solution(mesh):
    in_specs = (P(("wide", "narrow"), None), P(), P(("wide", "narrow")))
    out_specs = P("wide")
    return jax.shard_map(body, mesh=mesh, in_specs=in_specs, out_specs=out_specs, check_vma=False)
```

time: 214 us -> 35.7 us (0.17)
  blocking collectives: 110 us -> 0 us
  waiting for transfers between devices: 56.1 us -> 0 us
  Pallas kernels: 0 us -> 34.2 us
  matrix products: 16.3 us -> 0 us
  starting transfers between devices: 14 us -> 0 us
  between operations: 13.5 us -> 0.01 us
    all_gather x2 -> x0, blocking collectives: 110 us -> none  [the longest x1 85.4 us: body(): lax.all_gather(cluster_id, 'narrow', axis=0, tiled=True)]
    all_gather x1 -> x0, waiting for transfers between devices: 56.1 us -> none  [body(): lax.all_gather(unit, 'narrow', axis=0, tiled=True)]
    pallas_call x0 -> x1, Pallas kernels: none -> 34.2 us  [body(): pl.pallas_call(kernel, out_shape=jax.ShapeDtypeStruct((8, GROUPS, LANES),...]
    dot_general x5 -> x0, matrix products: 16.3 us -> none  [the longest x4 14.8 us: tile_max(): scores = jnp.dot(queries, keys.T, preferred_element_type=jnp.float32)]
    ppermute x8 -> x0, starting transfers between devices: 14 us -> none  [passed_along(): return lax.ppermute(block, axis, route)]
  transfers between devices with their start and end apart: 9 -> 0, of which waited for: 1 -> 0; matrix products, arithmetic and copies ran while one was open for 4% -> 0% of each run, Pallas kernels for 0% -> 0%
where the time goes in v2:
time: 35.7 us; the launch traced here: 35.5 us
  Pallas kernels  34.2 us (96%)
  local copies, waits for them, and re-layouts  1.32 us (4%)
    pallas_call x1, Pallas kernels, body(): pl.pallas_call(kernel, out_shape=jax.ShapeDtypeStruct((8, GROUPS, LANES),...  34.2 us
    unnamed x1, local copies, waits for them, and re-layouts  1.32 us

profile of v2, /device:TPU:2, one launch (start us, length us, event | category | flops | bytes accessed | tf_op | source)
XLA Modules:
  0.0 35.5 jit_solution(8916163606525966317)
XLA Ops:
  0.0 34.2 %best_match.1 = f32[8,4,128]{2,1,0:T(4,128)} custom-call(bf16[512,1024]{1,0:T(8,128)(2,1)} %emb.1, bf16[1024,256]{1,0:T(8,128)(2,1)} %proj.1, s32[4,128]{1,0:T(4,128)} %bitcast.3), custom_call_target="tpu_custom_call" | custom-call | tf_op jit(solution)/shard_map/best_match/pallas_call | solution.py:355
  34.2 1.3 %copy.5 = f32[4096]{0:T(1024)} copy(f32[4096]{0:T(1024)} %bitcast.2) | data formatting | bytes 32768

commit v3 on v2

v3 whole, which is shorter than its diff:
```python
import jax
import jax.numpy as jnp
from jax import lax
from jax.experimental import pallas as pl
from jax.experimental.pallas import tpu as pltpu
from jax.sharding import PartitionSpec as P

MESH = pl.DeviceIdType.MESH
ROWS = 512
SK = 256
D = 1024
CHUNKS = 4
CH = ROWS // CHUNKS
HALF = ROWS // 2
PLANES = 16
LANES = 128
GROUPS = ROWS // LANES


def device(plane, n, core):
    return (lax.rem(plane + PLANES, PLANES) * 2 + core, n)


def kernel(
    emb,
    proj,
    ids_in,
    out,
    emb_v,
    proj_v,
    ids,
    r_unit,
    s_unit,
    r_ids,
    s_ids,
    r_col,
    row_acc,
    col_acc,
    row_all,
    col_src,
    col_all,
    in_sem,
    y_send,
    relay_send,
    r_recv,
    p_send,
    f_send,
    q_send,
    s_recv,
    id_send,
    rid_recv,
    sid_recv,
    tail_send,
    tail_recv,
):
    wide, n = lax.axis_index("wide"), lax.axis_index("narrow")
    plane, core = wide // 2, lax.rem(wide, 2)
    y, x = n // 2, lax.rem(n, 2)
    n_x = y * 2 + 1 - x
    crosses_out = lax.rem(plane, 8) == 7
    crosses_in = lax.rem(plane, 8) == 0
    n_p = jnp.where(crosses_out, n_x, n)
    n_f = jnp.where(crosses_out, n, n_x)
    x_p = jnp.where(crosses_in, 1 - x, x)
    p_slot, f_slot = 2 * core, 2 + core

    proj_in = pltpu.make_async_copy(proj, proj_v, in_sem.at[2])
    proj_in.start()
    ids_copy = pltpu.make_async_copy(ids_in, ids, in_sem.at[3])
    emb_in = []
    for h in range(2):
        rows = pl.ds(h * HALF, HALF)
        emb_in.append(pltpu.make_async_copy(emb.at[rows], emb_v.at[rows], in_sem.at[h]))
        emb_in[h].start()
    ids_copy.start()

    barrier = pltpu.get_barrier_semaphore()

    def greet(where):
        pl.semaphore_signal(barrier, inc=1, device_id=where, device_id_type=MESH)

    for m in (n, n_x):
        greet(device(plane - 1, m, core))
        greet(device(plane - 1 + core, m, 1 - core))
    for k in range(1, 8):
        greet(device(plane, lax.rem(n + k, 8), core))
    for k in range(8):
        greet(device(plane + 1, k, core))
        greet(device(plane + core, k, 1 - core))

    def remote(src, dst, send, recv, where):
        return pltpu.make_async_remote_copy(
            src_ref=src,
            dst_ref=dst,
            send_sem=send,
            recv_sem=recv,
            device_id=where,
            device_id_type=MESH,
        )

    def piece(k):
        return pl.ds(k * CH, CH)

    def y_peer(d):
        return device(plane, lax.rem(y + d, 4) * 2 + x, core)

    def y_copy(d, k):
        slot = 2 if d == 1 else 1
        src, dst = r_unit.at[0, piece(k)], r_unit.at[slot, piece(k)]
        return remote(src, dst, y_send.at[slot - 1, k], r_recv.at[slot, k], y_peer(d))

    def relay_copy(slot, k):
        src, dst = r_unit.at[slot, piece(k)], r_unit.at[3, piece(k)]
        where = y_peer(3 if slot == 1 else 1)
        return remote(src, dst, relay_send.at[slot - 1, k % 2], r_recv.at[3, k], where)

    def p_copy(k):
        src, dst = r_unit.at[0, piece(k)], s_unit.at[p_slot, piece(k)]
        return remote(src, dst, p_send.at[k], s_recv.at[p_slot, k], device(plane + 1, n_p, core))

    def f_copy(k):
        src, dst = s_unit.at[p_slot, piece(k)], s_unit.at[f_slot, piece(k)]
        return remote(src, dst, f_send.at[k], s_recv.at[f_slot, k], device(plane, n_x, core))

    def q0_copy(i, k):
        src, dst = r_unit.at[0, piece(k)], s_unit.at[i, piece(k)]
        where = device(plane, n_x if i else n, 1)
        return remote(src, dst, q_send.at[i, k], s_recv.at[i, k], where)

    def q1_copy(i, k):
        src, dst = s_unit.at[2 + i, piece(k)], s_unit.at[1 + 2 * i, piece(k)]
        where = device(plane, n, 0)
        return remote(src, dst, q_send.at[i, k], s_recv.at[1 + 2 * i, k], where)

    def id_copies():
        copies = [
            remote(ids, r_ids.at[slot], id_send.at[slot - 1], rid_recv.at[slot], y_peer(d))
            for slot, d in ((3, 2), (2, 1), (1, 3))
        ]
        n_q = jnp.where(core == 0, n, n_p)
        n_r = jnp.where(core == 0, n_x, n_f)
        for i, (slot, where) in enumerate(
            (
                (p_slot, device(plane + 1, n_p, core)),
                (f_slot, device(plane + 1, n_f, core)),
                (core, device(plane + core, n_q, 1 - core)),
                (1 + 2 * core, device(plane + core, n_r, 1 - core)),
            )
        ):
            copies.append(remote(ids, s_ids.at[slot], id_send.at[3 + i], sid_recv.at[slot], where))
        return copies

    proj_in.wait()
    for h in range(2):
        emb_in[h].wait()
        rows = slice(h * HALF, (h + 1) * HALF)
        sketch = jnp.dot(emb_v[rows, :], proj_v[...], preferred_element_type=jnp.float32)
        squares = jnp.sum(sketch * sketch, axis=1, keepdims=True)
        r_unit[0, rows, :] = (sketch * lax.rsqrt(squares + 1e-06)).astype(jnp.bfloat16)
        if h == 0:
            pl.semaphore_wait(barrier, 27)
        near = (2 * h, 2 * h + 1)
        for k in near:
            p_copy(k).start()
            y_copy(1, k).start()
            if h == 1:
                y_copy(3, k).start()

        @pl.when(core == 0)
        def _():
            for k in near:
                q0_copy(1, k).start()
                q0_copy(0, k).start()

        if h == 0:
            y_copy(3, 0).start()
            ids_copy.wait()
            for copy in id_copies():
                copy.start()
        else:
            y_copy(3, 1).start()

    def columns(slot, rows):
        for j in range(GROUPS):
            row = rows[j : j + 1, :].astype(jnp.float32)
            r_col[slot, j * LANES : (j + 1) * LANES, :] = jnp.broadcast_to(row, (LANES, LANES)).T

    columns(0, ids[...])
    row_acc[...] = jnp.full_like(row_acc, -1.0)
    col_acc[...] = jnp.full_like(col_acc, -1.0)

    def landed(ref, sem):
        pltpu.make_async_copy(ref, ref, sem).wait()

    def r_wait(d, k):
        landed(r_unit.at[d, piece(k)], r_recv.at[d, k])

    def s_wait(s, k):
        landed(s_unit.at[s, piece(k)], s_recv.at[s, k])

    def to_core_0(i, k):
        @pl.when(core == 1)
        def _():
            q1_copy(i, k).start()

    for k in range(CHUNKS):
        if k < 2:
            for slot, piece_of in ((1, 2 + k), (2, k)):
                r_wait(slot, piece_of)
                relay_copy(slot, piece_of).start()
        s_wait(p_slot, k)
        f_copy(k).start()
        to_core_0(0, k)

    for slot in (1, 2, 3):
        landed(r_ids.at[slot], rid_recv.at[slot])
        columns(slot, r_ids[slot])
    for s in range(4):
        landed(s_ids.at[s], sid_recv.at[s])
    for k in range(2):
        r_wait(1, k)
        r_wait(2, 2 + k)

    def score(r, s, peaks, bests):
        scores = lax.dot_general(
            r_unit[r], s_unit[s], (((1,), (1,)), ((), ())), preferred_element_type=jnp.float32
        )
        a_ids = r_col[r]
        for j in range(GROUPS):
            b_ids = s_ids[s, pl.ds(j, 1), :].astype(jnp.float32)
            kept = jnp.where(a_ids == b_ids, scores[:, j * LANES : (j + 1) * LANES], -1.0)
            bests[r] = jnp.maximum(bests[r], kept)
            peaks[j] = jnp.maximum(peaks[j], jnp.max(kept.reshape(ROWS // 8, 8, LANES), axis=0))

    @pl.loop(0, 4)
    def _(s):
        @pl.when(jnp.logical_and(s != p_slot, s != 4 - core))
        def _():
            for k in range(CHUNKS):
                s_wait(s, k)

        @pl.when(jnp.logical_and(core == 1, s > 0))
        def _():
            s_wait(3, s)
            q1_copy(1, s).start()

        @pl.when(jnp.logical_and(core == 1, s == 1))
        def _():
            s_wait(3, 0)
            q1_copy(1, 0).start()

        peaks = [col_acc[s, j] for j in range(GROUPS)]
        bests = {r: row_acc[r] for r in range(3)}
        for r in range(3):
            score(r, s, peaks, bests)
            row_acc[r] = bests[r]
        for j in range(GROUPS):
            col_acc[s, j] = peaks[j]

    def rows_done(r, best):
        at = lax.rem(y + (0, 1, 3, 2)[r], 4)
        for j in range(GROUPS):
            part = best[j * LANES : (j + 1) * LANES, :].T
            row_all[n, at, j : j + 1, :] = jnp.max(part, axis=0, keepdims=True)

    for k in range(CHUNKS):
        r_wait(3, k)
    bests = {3: row_acc[3]}
    for s in range(4):
        peaks = [col_acc[s, j] for j in range(GROUPS)]
        score(3, s, peaks, bests)
        block = jnp.where(core == 0, s % 2, 1 - s // 2)
        x_0 = x_p if s < 2 else 1 - x_p
        x_1 = (x, 1 - x, x_p, 1 - x_p)[s]
        x_abs = jnp.where(core == 0, x_0, x_1)
        for j in range(GROUPS):
            col_src[block, x_abs, j : j + 1, :] = jnp.max(peaks[j], axis=0, keepdims=True)
        if s < 3:
            rows_done(s, row_acc[s])

    def tail(src, dst, kind, where):
        return remote(src, dst, tail_send.at[kind], tail_recv.at[kind], where)

    for k in range(8):
        tail(col_src.at[0], col_all.at[0, n], 1, device(plane - 1, k, core)).start()
        tail(col_src.at[1], col_all.at[1, n], 1, device(plane - 1 + core, k, 1 - core)).start()

    rows_done(3, bests[3])
    for k in range(1, 8):
        tail(row_all.at[n], row_all.at[n], 0, device(plane, lax.rem(n + k, 8), core)).start()

    some = row_all.at[pl.ds(0, 7)]
    landed(some, tail_recv.at[0])
    landed(col_all, tail_recv.at[1])
    for y_abs in range(4):
        for x_abs in range(2):
            best = jnp.full((GROUPS, LANES), -1.0, jnp.float32)
            for y_from in range(4):
                best = jnp.maximum(best, row_all[y_from * 2 + x_abs, y_abs])
            for g in range(2):
                for x_from in range(2):
                    best = jnp.maximum(best, col_all[g, y_abs * 2 + x_from, x_abs])
            out[y_abs * 2 + x_abs] = best

    landed(some, tail_send.at[0])
    landed(col_all, tail_send.at[1])
    for k in range(CHUNKS):
        y_copy(1, k).wait_send()
        y_copy(3, k).wait_send()
        relay_copy(1 if k >= 2 else 2, k).wait_send()
        p_copy(k).wait_send()
        f_copy(k).wait_send()
        for i in range(2):
            landed(r_unit.at[0, piece(k)], q_send.at[i, k])
    for copy in id_copies():
        copy.wait_send()


def body(embeddings, projection, cluster_id):
    dma = pltpu.SemaphoreType.DMA
    best = pl.pallas_call(
        kernel,
        out_shape=jax.ShapeDtypeStruct((8, GROUPS, LANES), jnp.float32),
        in_specs=[
            pl.BlockSpec(memory_space=pltpu.HBM),
            pl.BlockSpec(memory_space=pltpu.HBM),
            pl.BlockSpec(memory_space=pltpu.HBM),
        ],
        out_specs=pl.BlockSpec(memory_space=pltpu.VMEM),
        scratch_shapes=[
            pltpu.VMEM((ROWS, D), jnp.bfloat16),
            pltpu.VMEM((D, SK), jnp.bfloat16),
            pltpu.VMEM((GROUPS, LANES), jnp.int32),
            pltpu.VMEM((4, ROWS, SK), jnp.bfloat16),
            pltpu.VMEM((4, ROWS, SK), jnp.bfloat16),
            pltpu.VMEM((4, GROUPS, LANES), jnp.int32),
            pltpu.VMEM((4, GROUPS, LANES), jnp.int32),
            pltpu.VMEM((4, ROWS, LANES), jnp.float32),
            pltpu.VMEM((4, ROWS, LANES), jnp.float32),
            pltpu.VMEM((4, GROUPS, 8, LANES), jnp.float32),
            pltpu.VMEM((8, 4, GROUPS, LANES), jnp.float32),
            pltpu.VMEM((2, 2, GROUPS, LANES), jnp.float32),
            pltpu.VMEM((2, 8, 2, GROUPS, LANES), jnp.float32),
            dma((4,)),
            dma((2, CHUNKS)),
            dma((2, 2)),
            dma((4, CHUNKS)),
            dma((CHUNKS,)),
            dma((CHUNKS,)),
            dma((2, CHUNKS)),
            dma((4, CHUNKS)),
            dma((7,)),
            dma((4,)),
            dma((4,)),
            dma((2,)),
            dma((2,)),
        ],
        compiler_params=pltpu.CompilerParams(
            collective_id=0, has_side_effects=True, vmem_limit_bytes=62 << 20
        ),
        name="best_match",
    )(embeddings, projection, cluster_id.reshape(GROUPS, LANES))
    return best.reshape(8 * ROWS)


def solution(mesh):
    in_specs = (P(("wide", "narrow"), None), P(), P(("wide", "narrow")))
    out_specs = P("wide")
    return jax.shard_map(body, mesh=mesh, in_specs=in_specs, out_specs=out_specs, check_vma=False)
```

time: 35.7 us -> 31.7 us (0.89)
  the two profiles are of different devices: /device:TPU:2 before, /device:TPU:1 now
where the time goes in v3:
time: 31.7 us; the launch traced here: 31.5 us
  Pallas kernels  30.2 us (95%)
  local copies, waits for them, and re-layouts  1.32 us (4%)
    pallas_call x1, Pallas kernels, body(): pl.pallas_call(kernel, out_shape=jax.ShapeDtypeStruct((8, GROUPS, LANES),...  30.2 us
    unnamed x1, local copies, waits for them, and re-layouts  1.32 us

profile of v3, /device:TPU:1, one launch (start us, length us, event | category | flops | bytes accessed | tf_op | source)
XLA Modules:
  0.0 31.5 jit_solution(3263929100803096227)
XLA Ops:
  0.0 30.2 %best_match.1 = f32[8,4,128]{2,1,0:T(4,128)} custom-call(bf16[512,1024]{1,0:T(8,128)(2,1)} %emb.1, bf16[1024,256]{1,0:T(8,128)(2,1)} %proj.1, s32[4,128]{1,0:T(4,128)} %bitcast.3), custom_call_target="tpu_custom_call" | custom-call | tf_op jit(solution)/shard_map/best_match/pallas_call | solution.py:321
  30.2 1.3 %copy.5 = f32[4096]{0:T(1024)} copy(f32[4096]{0:T(1024)} %bitcast.2) | data formatting | bytes 32768

commit v4 on v3

v4 whole, which is shorter than its diff:
```python
import jax
import jax.numpy as jnp
from jax import lax
from jax.experimental import pallas as pl
from jax.experimental.pallas import tpu as pltpu
from jax.sharding import PartitionSpec as P

MESH = pl.DeviceIdType.MESH
ROWS = 512
SK = 256
D = 1024
CHUNKS = 4
CH = ROWS // CHUNKS
HALF = ROWS // 2
HEAD = 16
PLANES = 16
LANES = 128
GROUPS = ROWS // LANES


def device(plane, n, core):
    return (lax.rem(plane + PLANES, PLANES) * 2 + core, n)


def kernel(
    emb,
    proj,
    ids_in,
    out,
    emb_v,
    proj_v,
    ids,
    r_unit,
    s_unit,
    r_col,
    row_acc,
    col_acc,
    row_all,
    col_src,
    col_all,
    in_sem,
    y_send,
    relay_send,
    r_recv,
    p_send,
    f_send,
    q_send,
    s_recv,
    tail_send,
    tail_recv,
    ready,
):
    wide, n = lax.axis_index("wide"), lax.axis_index("narrow")
    plane, core = wide // 2, lax.rem(wide, 2)
    y, x = n // 2, lax.rem(n, 2)
    n_x = y * 2 + 1 - x
    crosses_out = lax.rem(plane, 8) == 7
    crosses_in = lax.rem(plane, 8) == 0
    n_p = jnp.where(crosses_out, n_x, n)
    n_from = jnp.where(crosses_in, n_x, n)
    x_p = jnp.where(crosses_in, 1 - x, x)
    p_slot, f_slot = 2 * core, 2 + core

    proj_in = pltpu.make_async_copy(proj, proj_v, in_sem.at[2])
    proj_in.start()
    ids_copy = pltpu.make_async_copy(ids_in, ids, in_sem.at[3])
    emb_in = []
    for h in range(2):
        rows = pl.ds(h * HALF, HALF)
        emb_in.append(pltpu.make_async_copy(emb.at[rows], emb_v.at[rows], in_sem.at[h]))
        emb_in[h].start()
    ids_copy.start()

    barrier = pltpu.get_barrier_semaphore()

    def greet(where):
        pl.semaphore_signal(barrier, inc=1, device_id=where, device_id_type=MESH)

    greet(device(plane - 1, n_from, core))
    greet(device(plane, lax.rem(y + 1, 4) * 2 + x, core))
    greet(device(plane, lax.rem(y + 3, 4) * 2 + x, core))
    greet(device(plane, n_x, core))
    greet(device(plane, n, 1 - core))

    @pl.when(core == 1)
    def _():
        greet(device(plane, n_x, 0))

    def remote(src, dst, send, recv, where):
        return pltpu.make_async_remote_copy(
            src_ref=src,
            dst_ref=dst,
            send_sem=send,
            recv_sem=recv,
            device_id=where,
            device_id_type=MESH,
        )

    def piece(k):
        return pl.ds(HEAD + k * CH, CH) if k else pl.ds(0, HEAD + CH)

    def y_peer(d):
        return device(plane, lax.rem(y + d, 4) * 2 + x, core)

    def y_copy(d, k):
        slot = 2 if d == 1 else 1
        src, dst = r_unit.at[0, piece(k)], r_unit.at[slot, piece(k)]
        return remote(src, dst, y_send.at[slot - 1, k], r_recv.at[slot, k], y_peer(d))

    def relay_copy(slot, k):
        src, dst = r_unit.at[slot, piece(k)], r_unit.at[3, piece(k)]
        where = y_peer(3 if slot == 1 else 1)
        return remote(src, dst, relay_send.at[slot - 1, k % 2], r_recv.at[3, k], where)

    def p_copy(k):
        src, dst = r_unit.at[0, piece(k)], s_unit.at[p_slot, piece(k)]
        return remote(src, dst, p_send.at[k], s_recv.at[p_slot, k], device(plane + 1, n_p, core))

    def f_copy(k):
        src, dst = s_unit.at[p_slot, piece(k)], s_unit.at[f_slot, piece(k)]
        return remote(src, dst, f_send.at[k], s_recv.at[f_slot, k], device(plane, n_x, core))

    def q0_copy(i, k):
        src, dst = r_unit.at[0, piece(k)], s_unit.at[i, piece(k)]
        where = device(plane, n_x if i else n, 1)
        return remote(src, dst, q_send.at[i, k], s_recv.at[i, k], where)

    def q1_copy(i, k):
        src, dst = s_unit.at[2 + i, piece(k)], s_unit.at[1 + 2 * i, piece(k)]
        where = device(plane, n, 0)
        return remote(src, dst, q_send.at[i, k], s_recv.at[1 + 2 * i, k], where)

    ids_copy.wait()
    clusters = jnp.concatenate(
        [ids[...].astype(jnp.float32), jnp.zeros((HEAD - GROUPS, LANES), jnp.float32)], axis=0
    )
    r_unit[0, :HEAD, :LANES] = clusters.astype(jnp.bfloat16)
    r_unit[0, :HEAD, LANES:] = jnp.zeros((HEAD, SK - LANES), jnp.bfloat16)
    proj_in.wait()
    for h in range(2):
        emb_in[h].wait()
        rows = slice(h * HALF, (h + 1) * HALF)
        sketch = jnp.dot(emb_v[rows, :], proj_v[...], preferred_element_type=jnp.float32)
        squares = jnp.sum(sketch * sketch, axis=1, keepdims=True)
        unit = (sketch * lax.rsqrt(squares + 1e-06)).astype(jnp.bfloat16)
        r_unit[0, HEAD + h * HALF : HEAD + (h + 1) * HALF, :] = unit
        if h == 0:
            pl.semaphore_wait(barrier, 6 - core)
        near = (2 * h, 2 * h + 1)
        for k in near:
            p_copy(k).start()
            y_copy(1, k).start()
            if h == 1:
                y_copy(3, k).start()
        y_copy(3, h).start()

        @pl.when(core == 0)
        def _():
            for k in near:
                if k < 3:
                    q0_copy(1, k).start()
                    q0_copy(0, k).start()

    def clusters_of(unit, slot):
        return unit[slot, :HEAD, :LANES].astype(jnp.float32)

    def columns(slot):
        rows = clusters_of(r_unit, slot)
        for j in range(GROUPS):
            row = jnp.broadcast_to(rows[j : j + 1, :], (LANES, LANES))
            r_col[slot, j * LANES : (j + 1) * LANES, :] = row.T

    columns(0)
    row_acc[...] = jnp.full_like(row_acc, -1.0)

    def landed(ref, sem):
        pltpu.make_async_copy(ref, ref, sem).wait()

    def r_wait(d, k):
        landed(r_unit.at[d, piece(k)], r_recv.at[d, k])

    def s_wait(s, k):
        landed(s_unit.at[s, piece(k)], s_recv.at[s, k])

    def to_core_0(i, k):
        @pl.when(core == 1)
        def _():
            q1_copy(i, k).start()

    for k in range(CHUNKS):
        if k < 2:
            for slot, piece_of in ((1, 2 + k), (2, k)):
                r_wait(slot, piece_of)
                relay_copy(slot, piece_of).start()
        if k == 0:

            @pl.when(core == 0)
            def _():
                q0_copy(1, 3).start()
                q0_copy(0, 3).start()

        s_wait(p_slot, k)
        f_copy(k).start()
        to_core_0(0, k)

    s_wait(f_slot, 0)
    pl.semaphore_signal(ready, inc=1, device_id=device(plane + 1, n_p, core), device_id_type=MESH)
    to_core_0(1, 0)
    for k in range(2):
        r_wait(1, k)
        r_wait(2, 2 + k)
    columns(1)
    columns(2)
    for k in range(CHUNKS):
        r_wait(3, k)
    columns(3)

    def arrive(s):
        @pl.when(jnp.logical_and(s != p_slot, s != 4 - core))
        def _():
            @pl.when(s != f_slot)
            def _():
                s_wait(s, 0)

            for k in range(1, CHUNKS):
                s_wait(s, k)

        for k in range(1, CHUNKS):

            @pl.when(jnp.logical_and(core == 1, s == k))
            def _():
                s_wait(3, k)
                if k == 3:
                    pl.semaphore_wait(ready, 1)
                q1_copy(1, k).start()

    def score(r, s, s_clusters, peaks, best):
        scores = lax.dot_general(
            r_unit[r, HEAD:],
            s_unit[s, HEAD:],
            (((1,), (1,)), ((), ())),
            preferred_element_type=jnp.float32,
        )
        a_ids = r_col[r]
        for j in range(GROUPS):
            lanes = slice(j * LANES, (j + 1) * LANES)
            kept = jnp.where(a_ids == s_clusters[j : j + 1, :], scores[:, lanes], -1.0)
            best = jnp.maximum(best, kept)
            peaks[j] = jnp.maximum(peaks[j], jnp.max(kept.reshape(ROWS // 8, 8, LANES), axis=0))
        return best

    @pl.loop(0, 3)
    def _(s):
        arrive(s)
        s_clusters = clusters_of(s_unit, s)
        peaks = [jnp.full((8, LANES), -1.0, jnp.float32)] * GROUPS
        for r in range(4):
            row_acc[r] = score(r, s, s_clusters, peaks, row_acc[r])
        for j in range(GROUPS):
            col_acc[s, j] = peaks[j]

    arrive(jnp.int32(3))
    s_clusters = clusters_of(s_unit, 3)
    peaks = [jnp.full((8, LANES), -1.0, jnp.float32)] * GROUPS
    for r in range(4):
        best = score(r, 3, s_clusters, peaks, row_acc[r])
        at = lax.rem(y + (0, 1, 3, 2)[r], 4)
        for j in range(GROUPS):
            part = best[j * LANES : (j + 1) * LANES, :].T
            row_all[n, at, j : j + 1, :] = jnp.max(part, axis=0, keepdims=True)

    def tail(src, dst, kind, where):
        return remote(src, dst, tail_send.at[kind], tail_recv.at[kind], where)

    for k in range(1, 8):
        tail(row_all.at[n], row_all.at[n], 0, device(plane, lax.rem(n + k, 8), core)).start()

    for s in range(4):
        block = jnp.where(core == 0, s % 2, 1 - s // 2)
        x_0 = x_p if s < 2 else 1 - x_p
        x_1 = (x, 1 - x, x_p, 1 - x_p)[s]
        x_abs = jnp.where(core == 0, x_0, x_1)
        for j in range(GROUPS):
            peak = peaks[j] if s == 3 else col_acc[s, j]
            col_src[block, x_abs, j : j + 1, :] = jnp.max(peak, axis=0, keepdims=True)

    @pl.when(core == 0)
    def _():
        pl.semaphore_wait(ready, 1)

    for k in range(8):
        tail(col_src.at[0], col_all.at[0, n], 1, device(plane - 1, k, core)).start()
        tail(col_src.at[1], col_all.at[1, n], 1, device(plane - 1 + core, k, 1 - core)).start()

    some = row_all.at[pl.ds(0, 7)]
    landed(some, tail_recv.at[0])
    landed(col_all, tail_recv.at[1])
    for y_abs in range(4):
        for x_abs in range(2):
            best = jnp.full((GROUPS, LANES), -1.0, jnp.float32)
            for y_from in range(4):
                best = jnp.maximum(best, row_all[y_from * 2 + x_abs, y_abs])
            for g in range(2):
                for x_from in range(2):
                    best = jnp.maximum(best, col_all[g, y_abs * 2 + x_from, x_abs])
            out[y_abs * 2 + x_abs] = best

    landed(some, tail_send.at[0])
    landed(col_all, tail_send.at[1])
    for k in range(CHUNKS):
        y_copy(1, k).wait_send()
        y_copy(3, k).wait_send()
        relay_copy(1 if k >= 2 else 2, k).wait_send()
        p_copy(k).wait_send()
        f_copy(k).wait_send()
        for i in range(2):
            landed(r_unit.at[0, piece(k)], q_send.at[i, k])


def body(embeddings, projection, cluster_id):
    dma = pltpu.SemaphoreType.DMA
    operands = embeddings, projection, cluster_id.reshape(GROUPS, LANES)
    best = pl.pallas_call(
        kernel,
        out_shape=jax.ShapeDtypeStruct((8, GROUPS, LANES), jnp.float32),
        in_specs=[
            pl.BlockSpec(memory_space=pltpu.HBM),
            pl.BlockSpec(memory_space=pltpu.HBM),
            pl.BlockSpec(memory_space=pltpu.HBM),
        ],
        out_specs=pl.BlockSpec(memory_space=pltpu.VMEM),
        scratch_shapes=[
            pltpu.VMEM((ROWS, D), jnp.bfloat16),
            pltpu.VMEM((D, SK), jnp.bfloat16),
            pltpu.VMEM((GROUPS, LANES), jnp.int32),
            pltpu.VMEM((4, HEAD + ROWS, SK), jnp.bfloat16),
            pltpu.VMEM((4, HEAD + ROWS, SK), jnp.bfloat16),
            pltpu.VMEM((4, ROWS, LANES), jnp.float32),
            pltpu.VMEM((4, ROWS, LANES), jnp.float32),
            pltpu.VMEM((4, GROUPS, 8, LANES), jnp.float32),
            pltpu.VMEM((8, 4, GROUPS, LANES), jnp.float32),
            pltpu.VMEM((2, 2, GROUPS, LANES), jnp.float32),
            pltpu.VMEM((2, 8, 2, GROUPS, LANES), jnp.float32),
            dma((4,)),
            dma((2, CHUNKS)),
            dma((2, 2)),
            dma((4, CHUNKS)),
            dma((CHUNKS,)),
            dma((CHUNKS,)),
            dma((2, CHUNKS)),
            dma((4, CHUNKS)),
            dma((2,)),
            dma((2,)),
            pltpu.SemaphoreType.REGULAR,
        ],
        compiler_params=pltpu.CompilerParams(
            collective_id=0, has_side_effects=True, vmem_limit_bytes=32 << 20
        ),
        name="best_match",
    )(*(pltpu.with_memory_space_constraint(a, pltpu.HBM) for a in operands))
    return best.reshape(8 * ROWS)


def solution(mesh):
    in_specs = (P(("wide", "narrow"), None), P(), P(("wide", "narrow")))
    out_specs = P("wide")
    return jax.shard_map(body, mesh=mesh, in_specs=in_specs, out_specs=out_specs, check_vma=False)
```

time: 31.7 us -> 27.3 us (0.86)
  the two profiles are of different devices: /device:TPU:1 before, /device:TPU:2 now
where the time goes in v4:
time: 27.3 us; the launch traced here: 27.2 us
  Pallas kernels  26.6 us (97%)
  local copies, waits for them, and re-layouts  0.61 us (2%)
    pallas_call x1, Pallas kernels, body(): pl.pallas_call(kernel, out_shape=jax.ShapeDtypeStruct((8, GROUPS, LANES),...  26.6 us
    unnamed x1, local copies, waits for them, and re-layouts  0.61 us

profile of v4, /device:TPU:2, one launch (start us, length us, event | category | flops | bytes accessed | tf_op | source)
XLA Modules:
  0.0 27.2 jit_solution(5874740020763152172)
XLA Ops:
  0.0 26.6 %best_match.1 = f32[8,4,128]{2,1,0:T(4,128)S(1)} custom-call(bf16[512,1024]{1,0:T(8,128)(2,1)} %emb.1, bf16[1024,256]{1,0:T(8,128)(2,1)} %proj.1, s32[4,128]{1,0:T(4,128)} %bitcast.3), custom_call_target="tpu_custom_call" | custom-call | tf_op jit(solution)/shard_map/best_match/pallas_call | solution.py:323
  26.6 0.6 %copy.5 = f32[4096]{0:T(1024)} copy(f32[4096]{0:T(1024)S(1)} %bitcast.2) | data formatting | bytes 32768

commit v5 on v4

--- a/solution.py
+++ b/solution.py
@@ -44,6 +44,7 @@
     r_recv,
     p_send,
     f_send,
+    d_send,
     q_send,
     s_recv,
     tail_send,
@@ -57,26 +58,27 @@
     crosses_out = lax.rem(plane, 8) == 7
     crosses_in = lax.rem(plane, 8) == 0
     n_p = jnp.where(crosses_out, n_x, n)
-    n_from = jnp.where(crosses_in, n_x, n)
+    n_f = jnp.where(crosses_out, n, n_x)
     x_p = jnp.where(crosses_in, 1 - x, x)
     p_slot, f_slot = 2 * core, 2 + core
 
-    proj_in = pltpu.make_async_copy(proj, proj_v, in_sem.at[2])
-    proj_in.start()
-    ids_copy = pltpu.make_async_copy(ids_in, ids, in_sem.at[3])
-    emb_in = []
-    for h in range(2):
-        rows = pl.ds(h * HALF, HALF)
-        emb_in.append(pltpu.make_async_copy(emb.at[rows], emb_v.at[rows], in_sem.at[h]))
-        emb_in[h].start()
-    ids_copy.start()
+    def load(src, dst, size, i, sem):
+        rows = pl.ds(i * size, size)
+        return pltpu.make_async_copy(src.at[rows], dst.at[rows], in_sem.at[sem])
+
+    ids_copy = pltpu.make_async_copy(ids_in, ids, in_sem.at[0])
+    emb_in = [load(emb, emb_v, CH, k, 1 + k) for k in range(4)]
+    proj_in = [load(proj, proj_v, D // 4, k, 5 + k) for k in range(4)]
+    for copy in (ids_copy, *proj_in, *emb_in):
+        copy.start()
 
     barrier = pltpu.get_barrier_semaphore()
 
     def greet(where):
         pl.semaphore_signal(barrier, inc=1, device_id=where, device_id_type=MESH)
 
-    greet(device(plane - 1, n_from, core))
+    greet(device(plane - 1, n, core))
+    greet(device(plane - 1, n_x, core))
     greet(device(plane, lax.rem(y + 1, 4) * 2 + x, core))
     greet(device(plane, lax.rem(y + 3, 4) * 2 + x, core))
     greet(device(plane, n_x, core))
@@ -120,6 +122,11 @@
         src, dst = s_unit.at[p_slot, piece(k)], s_unit.at[f_slot, piece(k)]
         return remote(src, dst, f_send.at[k], s_recv.at[f_slot, k], device(plane, n_x, core))
 
+    def d_copy():
+        src, dst = r_unit.at[0, piece(3)], s_unit.at[f_slot, piece(3)]
+        where = device(plane + 1, n_f, core)
+        return remote(src, dst, d_send.at[0], s_recv.at[f_slot, 3], where)
+
     def q0_copy(i, k):
         src, dst = r_unit.at[0, piece(k)], s_unit.at[i, piece(k)]
         where = device(plane, n_x if i else n, 1)
@@ -136,18 +143,22 @@
     )
     r_unit[0, :HEAD, :LANES] = clusters.astype(jnp.bfloat16)
     r_unit[0, :HEAD, LANES:] = jnp.zeros((HEAD, SK - LANES), jnp.bfloat16)
-    proj_in.wait()
+    for copy in proj_in:
+        copy.wait()
     for h in range(2):
-        emb_in[h].wait()
+        emb_in[2 * h].wait()
+        emb_in[2 * h + 1].wait()
         rows = slice(h * HALF, (h + 1) * HALF)
         sketch = jnp.dot(emb_v[rows, :], proj_v[...], preferred_element_type=jnp.float32)
         squares = jnp.sum(sketch * sketch, axis=1, keepdims=True)
         unit = (sketch * lax.rsqrt(squares + 1e-06)).astype(jnp.bfloat16)
         r_unit[0, HEAD + h * HALF : HEAD + (h + 1) * HALF, :] = unit
         if h == 0:
-            pl.semaphore_wait(barrier, 6 - core)
+            pl.semaphore_wait(barrier, 7 - core)
         near = (2 * h, 2 * h + 1)
         for k in near:
+            if k == 3:
+                d_copy().start()
             p_copy(k).start()
             y_copy(1, k).start()
             if h == 1:
@@ -200,7 +211,8 @@
                 q0_copy(0, 3).start()
 
         s_wait(p_slot, k)
-        f_copy(k).start()
+        if k < 3:
+            f_copy(k).start()
         to_core_0(0, k)
 
     s_wait(f_slot, 0)
@@ -312,7 +324,10 @@
         y_copy(3, k).wait_send()
         relay_copy(1 if k >= 2 else 2, k).wait_send()
         p_copy(k).wait_send()
-        f_copy(k).wait_send()
+        if k < 3:
+            f_copy(k).wait_send()
+        else:
+            d_copy().wait_send()
         for i in range(2):
             landed(r_unit.at[0, piece(k)], q_send.at[i, k])
 
@@ -341,12 +356,13 @@
             pltpu.VMEM((8, 4, GROUPS, LANES), jnp.float32),
             pltpu.VMEM((2, 2, GROUPS, LANES), jnp.float32),
             pltpu.VMEM((2, 8, 2, GROUPS, LANES), jnp.float32),
-            dma((4,)),
+            dma((9,)),
             dma((2, CHUNKS)),
             dma((2, 2)),
             dma((4, CHUNKS)),
             dma((CHUNKS,)),
-            dma((CHUNKS,)),
+            dma((CHUNKS - 1,)),
+            dma((1,)),
             dma((2, CHUNKS)),
             dma((4, CHUNKS)),
             dma((2,)),

time: 27.3 us -> 27.9 us (1.022)
  Pallas kernels: 26.6 us -> 27.2 us
    pallas_call x1, Pallas kernels: 26.6 us -> 27.2 us  [body(): pl.pallas_call(kernel, out_shape=jax.ShapeDtypeStruct((8, GROUPS, LANES),...]
where the time goes in v5:
time: 27.9 us; the launch traced here: 27.8 us
  Pallas kernels  27.2 us (97%)
  local copies, waits for them, and re-layouts  0.61 us (2%)
    pallas_call x1, Pallas kernels, body(): pl.pallas_call(kernel, out_shape=jax.ShapeDtypeStruct((8, GROUPS, LANES),...  27.2 us
    unnamed x1, local copies, waits for them, and re-layouts  0.61 us

profile of v5, /device:TPU:2, one launch (start us, length us, event | category | flops | bytes accessed | tf_op | source)
XLA Modules:
  0.0 27.8 jit_solution(18168546239896556767)
XLA Ops:
  0.0 27.2 %best_match.1 = f32[8,4,128]{2,1,0:T(4,128)S(1)} custom-call(bf16[512,1024]{1,0:T(8,128)(2,1)} %emb.1, bf16[1024,256]{1,0:T(8,128)(2,1)} %proj.1, s32[4,128]{1,0:T(4,128)} %bitcast.3), custom_call_target="tpu_custom_call" | custom-call | tf_op jit(solution)/shard_map/best_match/pallas_call | solution.py:338
  27.2 0.6 %copy.5 = f32[4096]{0:T(1024)} copy(f32[4096]{0:T(1024)S(1)} %bitcast.2) | data formatting | bytes 32768

commit v6 on v4

v6 whole, which is shorter than its diff:
```python
import jax
import jax.numpy as jnp
from jax import lax
from jax.experimental import pallas as pl
from jax.experimental.pallas import tpu as pltpu
from jax.sharding import PartitionSpec as P

MESH = pl.DeviceIdType.MESH
ROWS = 512
SK = 256
D = 1024
CHUNKS = 4
CH = ROWS // CHUNKS
HEAD = 16
UP = ((0, 144), (144, 128), (272, 64), (336, 64), (400, 128))
LAST = len(UP) - 1
PLANES = 16
LANES = 128
GROUPS = ROWS // LANES


def device(plane, n, core):
    return (lax.rem(plane + PLANES, PLANES) * 2 + core, n)


def kernel(
    emb,
    proj,
    ids_in,
    out,
    emb_v,
    proj_v,
    ids,
    r_unit,
    s_unit,
    r_col,
    row_acc,
    col_acc,
    row_all,
    col_src,
    col_all,
    in_sem,
    y_send,
    relay_send,
    r_recv,
    p_send,
    f_send,
    q_send,
    s_recv,
    tail_send,
    tail_recv,
    ready,
):
    wide, n = lax.axis_index("wide"), lax.axis_index("narrow")
    plane, core = wide // 2, lax.rem(wide, 2)
    y, x = n // 2, lax.rem(n, 2)
    n_x = y * 2 + 1 - x
    crosses_out = lax.rem(plane, 8) == 7
    crosses_in = lax.rem(plane, 8) == 0
    n_p = jnp.where(crosses_out, n_x, n)
    n_f = jnp.where(crosses_out, n, n_x)
    x_p = jnp.where(crosses_in, 1 - x, x)
    p_slot, f_slot = 2 * core, 2 + core

    first, rest = pl.ds(0, CH), pl.ds(CH, ROWS - CH)
    loads = [
        pltpu.make_async_copy(proj, proj_v, in_sem.at[0]),
        pltpu.make_async_copy(emb.at[first], emb_v.at[first], in_sem.at[1]),
        pltpu.make_async_copy(ids_in, ids, in_sem.at[2]),
        pltpu.make_async_copy(emb.at[rest], emb_v.at[rest], in_sem.at[3]),
    ]
    for copy in loads:
        copy.start()

    barrier = pltpu.get_barrier_semaphore()

    def greet(where):
        pl.semaphore_signal(barrier, inc=1, device_id=where, device_id_type=MESH)

    greet(device(plane - 1, n, core))
    greet(device(plane - 1, n_x, core))
    greet(device(plane, lax.rem(y + 1, 4) * 2 + x, core))
    greet(device(plane, lax.rem(y + 3, 4) * 2 + x, core))
    greet(device(plane, n_x, core))
    greet(device(plane, n, 1 - core))

    @pl.when(core == 1)
    def _():
        greet(device(plane, n_x, 0))

    def remote(src, dst, send, recv, where):
        return pltpu.make_async_remote_copy(
            src_ref=src,
            dst_ref=dst,
            send_sem=send,
            recv_sem=recv,
            device_id=where,
            device_id_type=MESH,
        )

    def piece(k):
        return pl.ds(HEAD + k * CH, CH) if k else pl.ds(0, HEAD + CH)

    def y_peer(d):
        return device(plane, lax.rem(y + d, 4) * 2 + x, core)

    def y_copy(d, k):
        slot = 2 if d == 1 else 1
        src, dst = r_unit.at[0, piece(k)], r_unit.at[slot, piece(k)]
        return remote(src, dst, y_send.at[slot - 1, k], r_recv.at[slot, k], y_peer(d))

    def relay_copy(slot, k):
        src, dst = r_unit.at[slot, piece(k)], r_unit.at[3, piece(k)]
        where = y_peer(3 if slot == 1 else 1)
        return remote(src, dst, relay_send.at[slot - 1, k % 2], r_recv.at[3, k], where)

    def up(k):
        return pl.ds(*UP[k])

    def p_copy(k):
        src, dst = r_unit.at[0, up(k)], s_unit.at[p_slot, up(k)]
        return remote(src, dst, p_send.at[k], s_recv.at[p_slot, k], device(plane + 1, n_p, core))

    def f_copy(k):
        here = s_unit.at[p_slot, up(k)] if k < LAST else r_unit.at[0, up(k)]
        where = device(plane, n_x, core) if k < LAST else device(plane + 1, n_f, core)
        return remote(here, s_unit.at[f_slot, up(k)], f_send.at[k], s_recv.at[f_slot, k], where)

    def q0_rows(k):
        return up(k) if k == LAST else pl.ds(0, UP[LAST][0])

    def q0_copy(i, k):
        src, dst = r_unit.at[0, q0_rows(k)], s_unit.at[i, q0_rows(k)]
        where = device(plane, n_x if i else n, 1)
        return remote(src, dst, q_send.at[i, k], s_recv.at[i, k], where)

    def q1_copy(i, k):
        src, dst = s_unit.at[2 + i, up(k)], s_unit.at[1 + 2 * i, up(k)]
        where = device(plane, n, 0)
        return remote(src, dst, q_send.at[i, k], s_recv.at[1 + 2 * i, k], where)

    loads[2].wait()
    clusters = jnp.concatenate(
        [ids[...].astype(jnp.float32), jnp.zeros((HEAD - GROUPS, LANES), jnp.float32)], axis=0
    )
    r_unit[0, :HEAD, :LANES] = clusters.astype(jnp.bfloat16)
    r_unit[0, :HEAD, LANES:] = jnp.zeros((HEAD, SK - LANES), jnp.bfloat16)

    def make_units(start, stop):
        sketch = jnp.dot(emb_v[start:stop, :], proj_v[...], preferred_element_type=jnp.float32)
        squares = jnp.sum(sketch * sketch, axis=1, keepdims=True)
        unit = (sketch * lax.rsqrt(squares + 1e-06)).astype(jnp.bfloat16)
        r_unit[0, HEAD + start : HEAD + stop, :] = unit

    loads[0].wait()
    loads[1].wait()
    make_units(0, CH)
    pl.semaphore_wait(barrier, 7 - core)
    p_copy(0).start()
    y_copy(1, 0).start()
    y_copy(3, 0).start()
    loads[3].wait()
    make_units(CH, ROWS)
    p_copy(1).start()
    y_copy(1, 1).start()
    y_copy(3, 2).start()
    p_copy(2).start()
    p_copy(3).start()
    y_copy(1, 2).start()
    y_copy(3, 3).start()
    p_copy(LAST).start()
    f_copy(LAST).start()
    y_copy(1, 3).start()
    y_copy(3, 1).start()

    @pl.when(core == 0)
    def _():
        q0_copy(1, 0).start()
        q0_copy(0, 0).start()

    def clusters_of(unit, slot):
        return unit[slot, :HEAD, :LANES].astype(jnp.float32)

    def columns(slot):
        rows = clusters_of(r_unit, slot)
        for j in range(GROUPS):
            row = jnp.broadcast_to(rows[j : j + 1, :], (LANES, LANES))
            r_col[slot, j * LANES : (j + 1) * LANES, :] = row.T

    columns(0)
    row_acc[...] = jnp.full_like(row_acc, -1.0)

    def landed(ref, sem):
        pltpu.make_async_copy(ref, ref, sem).wait()

    def r_wait(d, k):
        landed(r_unit.at[d, piece(k)], r_recv.at[d, k])

    def s_wait(s, k):
        landed(s_unit.at[s, up(k)], s_recv.at[s, k])

    def to_core_0(i, k):
        @pl.when(core == 1)
        def _():
            q1_copy(i, k).start()

    def hand_on(pieces):
        for k in pieces:
            s_wait(3, k)
            q1_copy(1, k).start()

    def score(r, s, s_clusters, peaks, best):
        scores = lax.dot_general(
            r_unit[r, HEAD:],
            s_unit[s, HEAD:],
            (((1,), (1,)), ((), ())),
            preferred_element_type=jnp.float32,
        )
        a_ids = r_col[r]
        for j in range(GROUPS):
            lanes = slice(j * LANES, (j + 1) * LANES)
            kept = jnp.where(a_ids == s_clusters[j : j + 1, :], scores[:, lanes], -1.0)
            best = jnp.maximum(best, kept)
            peaks[j] = jnp.maximum(peaks[j], jnp.max(kept.reshape(ROWS // 8, 8, LANES), axis=0))
        return best

    def rows_done(r, best):
        at = lax.rem(y + (0, 1, 3, 2)[r], 4)
        for j in range(GROUPS):
            part = best[j * LANES : (j + 1) * LANES, :].T
            row_all[n, at, j : j + 1, :] = jnp.max(part, axis=0, keepdims=True)

    def score_half(r, s, half, s_clusters, peaks, best):
        keys = pl.ds(pl.multiple_of(HEAD + half * (ROWS // 2), HEAD), ROWS // 2)
        scores = lax.dot_general(
            r_unit[r, HEAD:],
            s_unit[s, keys, :],
            (((1,), (1,)), ((), ())),
            preferred_element_type=jnp.float32,
        )
        a_ids = r_col[r]
        for j in range(GROUPS // 2):
            b_ids = jnp.where(half == 0, s_clusters[j : j + 1, :], s_clusters[j + 2 : j + 3, :])
            kept = jnp.where(a_ids == b_ids, scores[:, j * LANES : (j + 1) * LANES], -1.0)
            best = jnp.maximum(best, kept)
            peaks[j] = jnp.maximum(peaks[j], jnp.max(kept.reshape(ROWS // 8, 8, LANES), axis=0))
        return best

    def half_slot(s, half, done):
        s_clusters = clusters_of(s_unit, s)
        peaks = empty()[: GROUPS // 2]
        for r in range(4):
            done(r, score_half(r, s, half, s_clusters, peaks, row_acc[r]))
        for j in range(GROUPS // 2):
            col_acc[s, half * 2 + j] = peaks[j]

    def keep(r, best):
        row_acc[r] = best

    def score_near(s, peaks):
        s_clusters = clusters_of(s_unit, s)
        for r in range(3):
            row_acc[r] = score(r, s, s_clusters, peaks, row_acc[r])

    def empty():
        return [jnp.full((8, LANES), -1.0, jnp.float32)] * GROUPS

    def up_and_over(pieces):
        for k in pieces:
            s_wait(p_slot, k)
            f_copy(k).start()
            to_core_0(0, k)

    def say_ready():
        s_wait(f_slot, 0)
        pl.semaphore_signal(ready, inc=1, device_id=device(plane + 1, n_p, core), device_id_type=MESH)
        to_core_0(1, 0)

    def on_core(which, pieces, act):
        @pl.when(core == which)
        def _():
            for k in pieces:
                act(k)

    def relay(k):
        for slot, piece_of in ((2, k), (1, 2 + k)):
            r_wait(slot, piece_of)
            relay_copy(slot, piece_of).start()

    def late_q0():
        for i in (1, 0):
            q0_copy(i, LAST).start()

    def r_wait_near():
        for k in range(2):
            r_wait(1, k)
            r_wait(2, 2 + k)
        columns(1)
        columns(2)

    def r_wait_far():
        for k in range(CHUNKS):
            r_wait(3, k)
        columns(3)

    def q0_wait(s):
        for k in (0, LAST):
            landed(s_unit.at[s, q0_rows(k)], s_recv.at[s, k])

    @pl.when(crosses_in)
    def _():
        relay(0)
        on_core(0, (0,), lambda _: late_q0())
        relay(1)

        @pl.loop(0, 7)
        def _(i):
            @pl.when(i == 0)
            def _():
                up_and_over((0, 1))
                r_wait_near()
                r_wait_far()
                on_core(1, (0, 1), q0_wait)

            @pl.when(i == 1)
            def _():
                up_and_over((2, 3))
                on_core(0, (0, 1), lambda k: s_wait(1, k))

            @pl.when(i == 2)
            def _():
                say_ready()
                on_core(0, (LAST,), lambda k: s_wait(0, k))

            @pl.when(i == 3)
            def _():
                on_core(0, (2, 3, LAST), lambda k: s_wait(1, k))
                on_core(1, (LAST,), lambda k: s_wait(2, k))
                to_core_0(0, LAST)

            @pl.when(i == 4)
            def _():
                on_core(0, (1,), lambda k: s_wait(2, k))

            @pl.when(i == 5)
            def _():
                on_core(0, (0, 1), lambda k: s_wait(3, k))
                on_core(1, (0,), lambda _: hand_on((1, 2)))

            @pl.when(i == 6)
            def _():
                on_core(0, (2, 3, LAST), lambda k: s_wait(2, k))
                on_core(1, (0,), lambda _: hand_on((3,)))
                on_core(1, (0,), lambda _: pl.semaphore_wait(ready, 1))
                on_core(1, (0,), lambda _: hand_on((LAST,)))

            s = jnp.where(core == 0, 2 * (i // 4) + lax.rem(i, 2), i // 2)
            half = jnp.where(core == 0, lax.rem(i, 4) // 2, lax.rem(i, 2))
            half_slot(s, half, keep)

        on_core(0, (2, 3, LAST), lambda k: s_wait(3, k))
        half_slot(3, 1, rows_done)

    @pl.when(jnp.logical_not(crosses_in))
    def _():
        relay(0)
        up_and_over((0,))
        on_core(0, (0,), lambda _: late_q0())
        up_and_over((1,))
        relay(1)
        up_and_over((2, 3))
        say_ready()
        s_wait(p_slot, LAST)
        to_core_0(0, LAST)
        r_wait_near()

        @pl.loop(0, 2)
        def _(s):
            @pl.when(jnp.logical_and(core == 0, s == 1))
            def _():
                for k in range(LAST + 1):
                    s_wait(1, k)

            @pl.when(core == 1)
            def _():
                q0_wait(s)

            peaks = empty()
            score_near(s, peaks)
            for j in range(GROUPS):
                col_acc[s, j] = peaks[j]

        @pl.when(core == 1)
        def _():
            hand_on((1, 2))

        r_wait_far()
        best = row_acc[3]
        for s in range(2):
            peaks = [col_acc[s, j] for j in range(GROUPS)]
            best = score(3, s, clusters_of(s_unit, s), peaks, best)
            for j in range(GROUPS):
                col_acc[s, j] = peaks[j]
        row_acc[3] = best

        @pl.when(core == 0)
        def _():
            for k in range(1, LAST + 1):
                s_wait(2, k)

        @pl.when(core == 1)
        def _():
            hand_on((3,))
            pl.semaphore_wait(ready, 1)
            hand_on((LAST,))

        peaks = empty()
        score_near(2, peaks)
        row_acc[3] = score(3, 2, clusters_of(s_unit, 2), peaks, row_acc[3])
        for j in range(GROUPS):
            col_acc[2, j] = peaks[j]

        @pl.when(core == 0)
        def _():
            for k in range(LAST + 1):
                s_wait(3, k)

        s_clusters = clusters_of(s_unit, 3)
        peaks = empty()
        for r in range(4):
            rows_done(r, score(r, 3, s_clusters, peaks, row_acc[r]))
        for j in range(GROUPS):
            col_acc[3, j] = peaks[j]

    def tail(src, dst, kind, where):
        return remote(src, dst, tail_send.at[kind], tail_recv.at[kind], where)

    def send_rows():
        for m in (
            *(device(plane, lax.rem(y + d, 4) * 2 + 1 - x, core) for d in (2, 1, 3)),
            *(y_peer(d) for d in (2, 1, 3)),
            device(plane, n_x, core),
        ):
            tail(row_all.at[n], row_all.at[n], 0, m).start()

    @pl.when(crosses_in)
    def _():
        send_rows()

    for s in range(4):
        block = jnp.where(core == 0, s % 2, 1 - s // 2)
        x_0 = x_p if s < 2 else 1 - x_p
        x_1 = (x, 1 - x, x_p, 1 - x_p)[s]
        x_abs = jnp.where(core == 0, x_0, x_1)
        for j in range(GROUPS):
            peak = jnp.max(col_acc[s, j], axis=0, keepdims=True)
            col_src[block, x_abs, j : j + 1, :] = peak

    @pl.when(core == 0)
    def _():
        pl.semaphore_wait(ready, 1)

    for k in range(8):
        tail(col_src.at[0], col_all.at[0, n], 1, device(plane - 1, k, core)).start()
        tail(col_src.at[1], col_all.at[1, n], 1, device(plane - 1 + core, k, 1 - core)).start()

    @pl.when(jnp.logical_not(crosses_in))
    def _():
        send_rows()

    for k in range(CHUNKS):
        y_copy(1, k).wait_send()
        y_copy(3, k).wait_send()
        relay_copy(1 if k >= 2 else 2, k).wait_send()
    for k in range(LAST + 1):
        p_copy(k).wait_send()
        f_copy(k).wait_send()
    for i in range(2):

        @pl.when(core == 0)
        def _():
            q0_copy(i, 0).wait_send()
            q0_copy(i, LAST).wait_send()

        @pl.when(core == 1)
        def _():
            for k in range(LAST + 1):
                q1_copy(i, k).wait_send()

    some = row_all.at[pl.ds(0, 7)]
    landed(some, tail_recv.at[0])
    landed(col_all, tail_recv.at[1])
    for y_abs in range(4):
        for x_abs in range(2):
            best = jnp.full((GROUPS, LANES), -1.0, jnp.float32)
            for y_from in range(4):
                best = jnp.maximum(best, row_all[y_from * 2 + x_abs, y_abs])
            for g in range(2):
                for x_from in range(2):
                    best = jnp.maximum(best, col_all[g, y_abs * 2 + x_from, x_abs])
            out[y_abs * 2 + x_abs] = best

    landed(some, tail_send.at[0])
    landed(col_all, tail_send.at[1])


def body(embeddings, projection, cluster_id):
    dma = pltpu.SemaphoreType.DMA
    operands = embeddings, projection, cluster_id.reshape(GROUPS, LANES)
    best = pl.pallas_call(
        kernel,
        out_shape=jax.ShapeDtypeStruct((8, GROUPS, LANES), jnp.float32),
        in_specs=[
            pl.BlockSpec(memory_space=pltpu.HBM),
            pl.BlockSpec(memory_space=pltpu.HBM),
            pl.BlockSpec(memory_space=pltpu.HBM),
        ],
        out_specs=pl.BlockSpec(memory_space=pltpu.VMEM),
        scratch_shapes=[
            pltpu.VMEM((ROWS, D), jnp.bfloat16),
            pltpu.VMEM((D, SK), jnp.bfloat16),
            pltpu.VMEM((GROUPS, LANES), jnp.int32),
            pltpu.VMEM((4, HEAD + ROWS, SK), jnp.bfloat16),
            pltpu.VMEM((4, HEAD + ROWS, SK), jnp.bfloat16),
            pltpu.VMEM((4, ROWS, LANES), jnp.float32),
            pltpu.VMEM((4, ROWS, LANES), jnp.float32),
            pltpu.VMEM((4, GROUPS, 8, LANES), jnp.float32),
            pltpu.VMEM((8, 4, GROUPS, LANES), jnp.float32),
            pltpu.VMEM((2, 2, GROUPS, LANES), jnp.float32),
            pltpu.VMEM((2, 8, 2, GROUPS, LANES), jnp.float32),
            dma((4,)),
            dma((2, CHUNKS)),
            dma((2, 2)),
            dma((4, CHUNKS)),
            dma((LAST + 1,)),
            dma((LAST + 1,)),
            dma((2, LAST + 1)),
            dma((4, LAST + 1)),
            dma((2,)),
            dma((2,)),
            pltpu.SemaphoreType.REGULAR,
        ],
        compiler_params=pltpu.CompilerParams(
            collective_id=0, has_side_effects=True, vmem_limit_bytes=32 << 20
        ),
        name="best_match",
    )(*(pltpu.with_memory_space_constraint(a, pltpu.HBM) for a in operands))
    return best.reshape(8 * ROWS)


def solution(mesh):
    in_specs = (P(("wide", "narrow"), None), P(), P(("wide", "narrow")))
    out_specs = P("wide")
    return jax.shard_map(body, mesh=mesh, in_specs=in_specs, out_specs=out_specs, check_vma=False)
```

time: 27.3 us -> 26.7 us (0.978)
  Pallas kernels: 26.6 us -> 26 us
    pallas_call x1, Pallas kernels: 26.6 us -> 26 us  [body(): pl.pallas_call(kernel, out_shape=jax.ShapeDtypeStruct((8, GROUPS, LANES),...]
where the time goes in v6:
time: 26.7 us; the launch traced here: 26.6 us
  Pallas kernels  26 us (97%)
  local copies, waits for them, and re-layouts  0.61 us (2%)
    pallas_call x1, Pallas kernels, body(): pl.pallas_call(kernel, out_shape=jax.ShapeDtypeStruct((8, GROUPS, LANES),...  26 us
    unnamed x1, local copies, waits for them, and re-layouts  0.61 us

profile of v6, /device:TPU:2, one launch (start us, length us, event | category | flops | bytes accessed | tf_op | source)
XLA Modules:
  0.0 26.6 jit_solution(1363594929085371560)
XLA Ops:
  0.0 26.0 %best_match.1 = f32[8,4,128]{2,1,0:T(4,128)S(1)} custom-call(bf16[512,1024]{1,0:T(8,128)(2,1)} %emb.1, bf16[1024,256]{1,0:T(8,128)(2,1)} %proj.1, s32[4,128]{1,0:T(4,128)} %bitcast.3), custom_call_target="tpu_custom_call" | custom-call | tf_op jit(solution)/shard_map/best_match/pallas_call | solution.py:510
  26.0 0.6 %copy.5 = f32[4096]{0:T(1024)} copy(f32[4096]{0:T(1024)S(1)} %bitcast.2) | data formatting | bytes 32768

commit v7 on v6

--- a/solution.py
+++ b/solution.py
@@ -12,7 +12,7 @@
 CHUNKS = 4
 CH = ROWS // CHUNKS
 HEAD = 16
-UP = ((0, 144), (144, 128), (272, 64), (336, 64), (400, 128))
+UP = ((0, 144), (144, 128), (272, 96), (368, 64), (432, 96))
 LAST = len(UP) - 1
 PLANES = 16
 LANES = 128
@@ -50,6 +50,7 @@
     tail_send,
     tail_recv,
     ready,
+    seen,
 ):
     wide, n = lax.axis_index("wide"), lax.axis_index("narrow")
     plane, core = wide // 2, lax.rem(wide, 2)
@@ -162,21 +163,20 @@
     loads[3].wait()
     make_units(CH, ROWS)
     p_copy(1).start()
+    p_copy(2).start()
+    p_copy(3).start()
+    p_copy(LAST).start()
+    f_copy(LAST).start()
     y_copy(1, 1).start()
     y_copy(3, 2).start()
-    p_copy(2).start()
-    p_copy(3).start()
     y_copy(1, 2).start()
     y_copy(3, 3).start()
-    p_copy(LAST).start()
-    f_copy(LAST).start()
     y_copy(1, 3).start()
     y_copy(3, 1).start()
 
     @pl.when(core == 0)
     def _():
         q0_copy(1, 0).start()
-        q0_copy(0, 0).start()
 
     def clusters_of(unit, slot):
         return unit[slot, :HEAD, :LANES].astype(jnp.float32)
@@ -271,10 +271,12 @@
             f_copy(k).start()
             to_core_0(0, k)
 
+    def tell(sem, where):
+        pl.semaphore_signal(sem, inc=1, device_id=where, device_id_type=MESH)
+
     def say_ready():
-        s_wait(f_slot, 0)
-        pl.semaphore_signal(ready, inc=1, device_id=device(plane + 1, n_p, core), device_id_type=MESH)
-        to_core_0(1, 0)
+        pl.semaphore_wait(seen, 1)
+        tell(ready, device(plane + 1, n_p, core))
 
     def on_core(which, pieces, act):
         @pl.when(core == which)
@@ -290,6 +292,7 @@
     def late_q0():
         for i in (1, 0):
             q0_copy(i, LAST).start()
+        q0_copy(0, 0).start()
 
     def r_wait_near():
         for k in range(2):
@@ -310,8 +313,10 @@
     @pl.when(crosses_in)
     def _():
         relay(0)
+        tell(seen, device(plane, n_x, core))
         on_core(0, (0,), lambda _: late_q0())
         relay(1)
+        say_ready()
 
         @pl.loop(0, 7)
         def _(i):
@@ -329,7 +334,8 @@
 
             @pl.when(i == 2)
             def _():
-                say_ready()
+                s_wait(f_slot, 0)
+                to_core_0(1, 0)
                 on_core(0, (LAST,), lambda k: s_wait(0, k))
 
             @pl.when(i == 3)
@@ -364,12 +370,15 @@
     @pl.when(jnp.logical_not(crosses_in))
     def _():
         relay(0)
+        tell(seen, device(plane, n_x, core))
         up_and_over((0,))
         on_core(0, (0,), lambda _: late_q0())
         up_and_over((1,))
         relay(1)
         up_and_over((2, 3))
         say_ready()
+        s_wait(f_slot, 0)
+        to_core_0(1, 0)
         s_wait(p_slot, LAST)
         to_core_0(0, LAST)
         r_wait_near()
@@ -539,6 +548,7 @@
             dma((2,)),
             dma((2,)),
             pltpu.SemaphoreType.REGULAR,
+            pltpu.SemaphoreType.REGULAR,
         ],
         compiler_params=pltpu.CompilerParams(
             collective_id=0, has_side_effects=True, vmem_limit_bytes=32 << 20

time: 26.7 us -> 26.4 us (0.989)
  Pallas kernels: 26 us -> 25.7 us
    pallas_call x1, Pallas kernels: 26 us -> 25.7 us  [body(): pl.pallas_call(kernel, out_shape=jax.ShapeDtypeStruct((8, GROUPS, LANES),...]
where the time goes in v7:
time: 26.4 us; the launch traced here: 26.3 us
  Pallas kernels  25.7 us (97%)
  local copies, waits for them, and re-layouts  0.61 us (2%)
    pallas_call x1, Pallas kernels, body(): pl.pallas_call(kernel, out_shape=jax.ShapeDtypeStruct((8, GROUPS, LANES),...  25.7 us
    unnamed x1, local copies, waits for them, and re-layouts  0.61 us

profile of v7, /device:TPU:2, one launch (start us, length us, event | category | flops | bytes accessed | tf_op | source)
XLA Modules:
  0.0 26.3 jit_solution(14661945520572128318)
XLA Ops:
  0.0 25.7 %best_match.1 = f32[8,4,128]{2,1,0:T(4,128)S(1)} custom-call(bf16[512,1024]{1,0:T(8,128)(2,1)} %emb.1, bf16[1024,256]{1,0:T(8,128)(2,1)} %proj.1, s32[4,128]{1,0:T(4,128)} %bitcast.3), custom_call_target="tpu_custom_call" | custom-call | tf_op jit(solution)/shard_map/best_match/pallas_call | solution.py:519
  25.7 0.6 %copy.5 = f32[4096]{0:T(1024)} copy(f32[4096]{0:T(1024)S(1)} %bitcast.2) | data formatting | bytes 32768

commit v8 on v7

--- a/solution.py
+++ b/solution.py
@@ -318,7 +318,7 @@
         relay(1)
         say_ready()
 
-        @pl.loop(0, 7)
+        @pl.loop(0, 6)
         def _(i):
             @pl.when(i == 0)
             def _():
@@ -353,19 +353,24 @@
                 on_core(0, (0, 1), lambda k: s_wait(3, k))
                 on_core(1, (0,), lambda _: hand_on((1, 2)))
 
-            @pl.when(i == 6)
-            def _():
-                on_core(0, (2, 3, LAST), lambda k: s_wait(2, k))
-                on_core(1, (0,), lambda _: hand_on((3,)))
-                on_core(1, (0,), lambda _: pl.semaphore_wait(ready, 1))
-                on_core(1, (0,), lambda _: hand_on((LAST,)))
-
-            s = jnp.where(core == 0, 2 * (i // 4) + lax.rem(i, 2), i // 2)
-            half = jnp.where(core == 0, lax.rem(i, 4) // 2, lax.rem(i, 2))
+            by_slot = jnp.logical_and(core == 1, i < 4)
+            s = jnp.where(by_slot, i // 2, 2 * (i // 4) + lax.rem(i, 2))
+            half = jnp.where(by_slot, lax.rem(i, 2), lax.rem(i, 4) // 2)
             half_slot(s, half, keep)
 
-        on_core(0, (2, 3, LAST), lambda k: s_wait(3, k))
-        half_slot(3, 1, rows_done)
+        on_core(1, (0,), lambda _: hand_on((3,)))
+        on_core(1, (0,), lambda _: pl.semaphore_wait(ready, 1))
+        on_core(1, (0,), lambda _: hand_on((LAST,)))
+        for slot in (2, 3):
+            on_core(0, (2, 3, LAST), lambda k, slot=slot: s_wait(slot, k))
+        peaks = [empty()[: GROUPS // 2] for _ in range(2)]
+        clusters_2, clusters_3 = clusters_of(s_unit, 2), clusters_of(s_unit, 3)
+        for r in range(4):
+            best = score_half(r, 2, 1, clusters_2, peaks[0], row_acc[r])
+            rows_done(r, score_half(r, 3, 1, clusters_3, peaks[1], best))
+        for i in range(2):
+            for j in range(GROUPS // 2):
+                col_acc[2 + i, 2 + j] = peaks[i][j]
 
     @pl.when(jnp.logical_not(crosses_in))
     def _():
@@ -452,9 +457,7 @@
         ):
             tail(row_all.at[n], row_all.at[n], 0, m).start()
 
-    @pl.when(crosses_in)
-    def _():
-        send_rows()
+    send_rows()
 
     for s in range(4):
         block = jnp.where(core == 0, s % 2, 1 - s // 2)
@@ -473,9 +476,6 @@
         tail(col_src.at[0], col_all.at[0, n], 1, device(plane - 1, k, core)).start()
         tail(col_src.at[1], col_all.at[1, n], 1, device(plane - 1 + core, k, 1 - core)).start()
 
-    @pl.when(jnp.logical_not(crosses_in))
-    def _():
-        send_rows()
 
     for k in range(CHUNKS):
         y_copy(1, k).wait_send()

time: 26.4 us -> 26 us (0.985)
  Pallas kernels: 25.7 us -> 25.3 us
    pallas_call x1, Pallas kernels: 25.7 us -> 25.3 us  [body(): pl.pallas_call(kernel, out_shape=jax.ShapeDtypeStruct((8, GROUPS, LANES),...]
where the time goes in v8:
time: 26 us
  Pallas kernels  25.3 us (97%)
  local copies, waits for them, and re-layouts  0.61 us (2%)
    pallas_call x1, Pallas kernels, body(): pl.pallas_call(kernel, out_shape=jax.ShapeDtypeStruct((8, GROUPS, LANES),...  25.3 us
    unnamed x1, local copies, waits for them, and re-layouts  0.61 us

profile of v8, /device:TPU:2, one launch (start us, length us, event | category | flops | bytes accessed | tf_op | source)
XLA Modules:
  0.0 26.0 jit_solution(8633811187456653703)
XLA Ops:
  0.0 25.3 %best_match.1 = f32[8,4,128]{2,1,0:T(4,128)S(1)} custom-call(bf16[512,1024]{1,0:T(8,128)(2,1)} %emb.1, bf16[1024,256]{1,0:T(8,128)(2,1)} %proj.1, s32[4,128]{1,0:T(4,128)} %bitcast.3), custom_call_target="tpu_custom_call" | custom-call | tf_op jit(solution)/shard_map/best_match/pallas_call | solution.py:519
  25.3 0.6 %copy.5 = f32[4096]{0:T(1024)} copy(f32[4096]{0:T(1024)S(1)} %bitcast.2) | data formatting | bytes 32768

commit v9 on v8

--- a/solution.py
+++ b/solution.py
@@ -159,7 +159,6 @@
     pl.semaphore_wait(barrier, 7 - core)
     p_copy(0).start()
     y_copy(1, 0).start()
-    y_copy(3, 0).start()
     loads[3].wait()
     make_units(CH, ROWS)
     p_copy(1).start()
@@ -167,10 +166,11 @@
     p_copy(3).start()
     p_copy(LAST).start()
     f_copy(LAST).start()
+    y_copy(3, 2).start()
     y_copy(1, 1).start()
-    y_copy(3, 2).start()
+    y_copy(3, 3).start()
     y_copy(1, 2).start()
-    y_copy(3, 3).start()
+    y_copy(3, 0).start()
     y_copy(1, 3).start()
     y_copy(3, 1).start()
 
@@ -378,8 +378,8 @@
         tell(seen, device(plane, n_x, core))
         up_and_over((0,))
         on_core(0, (0,), lambda _: late_q0())
+        relay(1)
         up_and_over((1,))
-        relay(1)
         up_and_over((2, 3))
         say_ready()
         s_wait(f_slot, 0)

time: 26 us -> 26 us (level)
  no operation moved by 1% of the time
where the time goes in v9:
time: 26 us
  Pallas kernels  25.3 us (97%)
  local copies, waits for them, and re-layouts  0.61 us (2%)
    pallas_call x1, Pallas kernels, body(): pl.pallas_call(kernel, out_shape=jax.ShapeDtypeStruct((8, GROUPS, LANES),...  25.3 us
    unnamed x1, local copies, waits for them, and re-layouts  0.61 us

profile of v9, /device:TPU:2, one launch (start us, length us, event | category | flops | bytes accessed | tf_op | source)
XLA Modules:
  0.0 26.0 jit_solution(10668704113748014528)
XLA Ops:
  0.0 25.3 %best_match.1 = f32[8,4,128]{2,1,0:T(4,128)S(1)} custom-call(bf16[512,1024]{1,0:T(8,128)(2,1)} %emb.1, bf16[1024,256]{1,0:T(8,128)(2,1)} %proj.1, s32[4,128]{1,0:T(4,128)} %bitcast.3), custom_call_target="tpu_custom_call" | custom-call | tf_op jit(solution)/shard_map/best_match/pallas_call | solution.py:519
  25.3 0.6 %copy.5 = f32[4096]{0:T(1024)} copy(f32[4096]{0:T(1024)S(1)} %bitcast.2) | data formatting | bytes 32768

commit v10 on v9

--- a/solution.py
+++ b/solution.py
@@ -12,7 +12,7 @@
 CHUNKS = 4
 CH = ROWS // CHUNKS
 HEAD = 16
-UP = ((0, 144), (144, 128), (272, 96), (368, 64), (432, 96))
+UP = ((0, 144), (144, 128), (272, 112), (384, 80), (464, 64))
 LAST = len(UP) - 1
 PLANES = 16
 LANES = 128

time: 26 us -> 26 us (level)
  no operation moved by 1% of the time
where the time goes in v10:
time: 26 us; the launch traced here: 25.9 us
  Pallas kernels  25.3 us (97%)
  local copies, waits for them, and re-layouts  0.61 us (2%)
    pallas_call x1, Pallas kernels, body(): pl.pallas_call(kernel, out_shape=jax.ShapeDtypeStruct((8, GROUPS, LANES),...  25.3 us
    unnamed x1, local copies, waits for them, and re-layouts  0.61 us

profile of v10, /device:TPU:2, one launch (start us, length us, event | category | flops | bytes accessed | tf_op | source)
XLA Modules:
  0.0 25.9 jit_solution(4468076458697038061)
XLA Ops:
  0.0 25.3 %best_match.1 = f32[8,4,128]{2,1,0:T(4,128)S(1)} custom-call(bf16[512,1024]{1,0:T(8,128)(2,1)} %emb.1, bf16[1024,256]{1,0:T(8,128)(2,1)} %proj.1, s32[4,128]{1,0:T(4,128)} %bitcast.3), custom_call_target="tpu_custom_call" | custom-call | tf_op jit(solution)/shard_map/best_match/pallas_call | solution.py:519
  25.3 0.6 %copy.5 = f32[4096]{0:T(1024)} copy(f32[4096]{0:T(1024)S(1)} %bitcast.2) | data formatting | bytes 32768
